TPU v7x, 128 devices: a whole 4x4x4 slice. The times are simulated.
128 devices in a mesh: grp: 4 (over z), fsdp: 32 (over x, y, core).
Axes of the slice: x: 4, y: 4, z: 4, core: 2. Of those that a mesh axis runs over, the one named last changes fastest.
Arguments:
- tokens: bfloat16 [32768, 8192], P(('grp', 'fsdp')), may hold values from -6 to 6
- tenant: int32 [32768], P(('grp', 'fsdp')), may hold values from 0 to 511, as said below
- slot_table: int32 [4, 8], replicated, may hold values from 0 to 511, as said below
- weight: bfloat16 [8192, 1024], P('fsdp'), may hold values from -0.0625 to 0.0625
- adapter_a: bfloat16 [512, 524288], P('grp', 'fsdp'), may hold values from -0.0625 to 0.0625
- adapter_b: bfloat16 [512, 65536], P('grp', 'fsdp'), may hold values from -0.75 to 0.75
- cotangent: bfloat16 [32768, 1024], P(('grp', 'fsdp')), may hold values from -6 to 6
Outputs:
- output: bfloat16 [32768, 1024], P(('grp', 'fsdp'))
- token_grad: bfloat16 [32768, 8192], P(('grp', 'fsdp'))
- grad_a: bfloat16 [512, 524288], P('grp', 'fsdp')
- grad_b: bfloat16 [512, 65536], P('grp', 'fsdp')
Inputs may be any that keep to these rules, and one draw needn't show every extreme that they name: `slot_table`: row g lists 8 distinct adapters; its entries k * 2 to k * 2 + 1 are adapters of owner block k, that is ids from k * 128 to (k + 1) * 128 - 1. `tenant`: each row's adapter is one listed in its group's row of slot_table, and every listed adapter is used by some row of that group.
All inputs are finite; a program needn't handle non-finite values.
Results may differ from a plain program's by a relative error of at most 0.019.
Values may be sent and summed in bfloat16 or wider, within the bound.
A program may use at most 128 MiB of HBM per device.

v0:
```python
import math

import jax
import jax.numpy as jnp
from jax import lax
from jax.sharding import PartitionSpec as P

SCALE = 2.0


def contract_last(left, right):
    return lax.dot_general(
        left, right, (((1,), (1,)), ((), ())), preferred_element_type=jnp.float32
    )


def contract_first(left, right):
    return lax.dot_general(
        left, right, (((0,), (0,)), ((), ())), preferred_element_type=jnp.float32
    )


def local(tokens, tenant, slot_table, weight, adapter_a, adapter_b, cotangent):
    row_count, width = tokens.shape
    out_width = weight.shape[1]
    group_count = lax.axis_size("grp")
    part_count = lax.axis_size("fsdp")
    group_id = lax.axis_index("grp")
    slot_count = slot_table.shape[1]
    per_owner = slot_count // group_count
    owned_count = adapter_a.shape[0]
    width_a = adapter_a.shape[1]
    width_b = adapter_b.shape[1]
    rank_size = width_a * part_count // width
    own_slots = lax.dynamic_index_in_dim(slot_table, group_id, 0, keepdims=False)
    wanted = (
        lax.dynamic_slice_in_dim(slot_table, group_id * per_owner, per_owner, 1)
        - group_id * owned_count
    )
    chosen_a = jnp.take(adapter_a, wanted, axis=0)
    chosen_b = jnp.take(adapter_b, wanted, axis=0)
    whole_a, whole_b = (
        lax.all_gather(chosen_a, "fsdp", axis=2, tiled=True),
        lax.all_gather(chosen_b, "fsdp", axis=2, tiled=True),
    )
    landed_a, landed_b = (
        lax.all_to_all(whole_a, "grp", split_axis=0, concat_axis=0, tiled=True),
        lax.all_to_all(whole_b, "grp", split_axis=0, concat_axis=0, tiled=True),
    )
    full_a = landed_a.reshape(slot_count, width_a * part_count)
    full_b = landed_b.reshape(slot_count, width_b * part_count)
    stack_a = full_a.reshape(slot_count * rank_size, width)
    stack_b = full_b.reshape(slot_count * rank_size, out_width)
    row_mask = jnp.repeat(
        (tenant[:, None] == own_slots[None, :]).astype(jnp.float32), rank_size, axis=1
    )
    low_proj = (contract_last(tokens, stack_a) * row_mask).astype(jnp.bfloat16)
    back_proj = (SCALE * row_mask * contract_last(cotangent, stack_b)).astype(jnp.bfloat16)
    full_weight = lax.all_gather(weight, "fsdp", axis=0, tiled=True)
    base_out = jnp.dot(tokens, full_weight, preferred_element_type=jnp.float32)
    dx_trunk = contract_last(cotangent, full_weight)
    output = (
        base_out + SCALE * jnp.dot(low_proj, stack_b, preferred_element_type=jnp.float32)
    ).astype(jnp.bfloat16)
    token_grad = (
        dx_trunk + jnp.dot(back_proj, stack_a, preferred_element_type=jnp.float32)
    ).astype(jnp.bfloat16)
    row_scale = 1.0 / math.sqrt(row_count * part_count)
    term_a = contract_first(back_proj, tokens) * row_scale
    term_b = contract_first(low_proj, cotangent) * (SCALE * row_scale)
    summed_a, summed_b = (
        lax.psum_scatter(
            term_a.reshape(slot_count, rank_size, width).astype(jnp.bfloat16),
            "fsdp",
            scatter_dimension=1,
            tiled=True,
        ).astype(jnp.float32),
        lax.psum_scatter(
            term_b.reshape(slot_count, rank_size, out_width).astype(jnp.bfloat16),
            "fsdp",
            scatter_dimension=1,
            tiled=True,
        ).astype(jnp.float32),
    )
    home_a, home_b = (
        lax.all_to_all(
            summed_a.reshape(group_count, per_owner, width_a).astype(jnp.bfloat16),
            "grp",
            split_axis=0,
            concat_axis=0,
            tiled=True,
        ).astype(jnp.float32),
        lax.all_to_all(
            summed_b.reshape(group_count, per_owner, width_b).astype(jnp.bfloat16),
            "grp",
            split_axis=0,
            concat_axis=0,
            tiled=True,
        ).astype(jnp.float32),
    )
    owner_hits = (
        jnp.arange(owned_count, dtype=jnp.int32)[:, None] == wanted.reshape(1, -1)
    ).astype(jnp.float32)
    grad_a = jnp.dot(
        owner_hits,
        home_a.reshape(group_count * per_owner, width_a),
        precision=lax.Precision.HIGHEST,
        preferred_element_type=jnp.float32,
    ).astype(jnp.bfloat16)
    grad_b = jnp.dot(
        owner_hits,
        home_b.reshape(group_count * per_owner, width_b),
        precision=lax.Precision.HIGHEST,
        preferred_element_type=jnp.float32,
    ).astype(jnp.bfloat16)
    return (output, token_grad, grad_a, grad_b)


def solution(mesh):
    return jax.shard_map(
        local,
        mesh=mesh,
        in_specs=(
            P(("grp", "fsdp"), None),
            P(("grp", "fsdp")),
            P(),
            P("fsdp", None),
            P("grp", "fsdp"),
            P("grp", "fsdp"),
            P(("grp", "fsdp"), None),
        ),
        out_specs=(
            P(("grp", "fsdp"), None),
            P(("grp", "fsdp"), None),
            P("grp", "fsdp"),
            P("grp", "fsdp"),
        ),
        check_vma=False,
    )
```

profile of v0, /device:TPU:1, one launch (start us, length us, event | category | flops | bytes accessed | tf_op | source)
XLA Modules:
  0.0 415.1 jit_solution(7790547578453710742)
XLA Ops:
  7.2 0.0 all-gather.8.cloned.1.call-start
  7.2 0.8 compare_and_fusion
  8.0 0.1 reshape.38
  8.1 1.7 gather_fusion.1
  9.9 0.7 broadcast_select_fusion.1
  10.6 0.0 all-gather.8.cloned.1.call-update
  10.6 0.0 all-gather.6.cloned.1.call-start
  10.7 3.7 gather_fusion
  14.4 0.2 reshape.37
  14.5 1.0 broadcast_select_fusion
  15.5 0.0 all-gather.6.cloned.1.call-update
  15.6 41.7 %all-gather.8.cloned.1.call-done = bf16[4,2,65536]{2,1,0:T(2,128)(2,1)} async-done(((bf16[4,2,2048]{2,1,0:T(2,128)(2,1)}), bf16[4,2,65536]{2,1,0:T(2,128)(2,1)}) %all-gather.8.cloned.1.call-update) | async-done | bytes 1048592 | tf_op jit(solution)/shard_map/all_gather | solution.py:44
  57.3 4.1 all-to-all-start.1
  61.4 0.7 dynamic-slice_bitcast_fusion
  62.1 0.7 compare_convert_fusion
  62.9 13.2 %all-to-all-done.1 = bf16[4,2,65536]{2,1,0:T(2,128)(2,1)S(1)} async-done(((bf16[4,2,65536]{2,1,0:T(2,128)(2,1)}), bf16[4,2,65536]{2,1,0:T(2,128)(2,1)S(1)}, u32[]{:S(2)}, u32[]{:S(2)}) %all-to-all-start.1) | async-done | bytes 1048608 | tf_op jit(solution)/shard_map/all_to_all | solution.py:48
  76.1 0.9 reshape_reshape.7
  77.0 0.5 fusion.5
  77.5 7.9 %multiply_convert_fusion = bf16[512,8192]{1,0:T(8,128)(2,1)} fusion(bf16[256,512]{0,1:T(8,128)(2,1)S(1)} %fusion.5, bf16[256,8192]{1,0:T(8,128)(2,1)} %param.7), kind=kOutput, calls=%fused_computation.3 | convolution fusion | flops 2155872256 | bytes 12845056 | tf_op jit(solution)/shard_map/dot_general | solution.py:18
  85.3 11.2 %copy.13 = bf16[8,64,8192]{2,0,1:T(8,128)(2,1)} copy(bf16[8,64,8192]{2,1,0:T(8,128)(2,1)} %bitcast.36) | data formatting | bytes 16777216 | tf_op jit(solution)/shard_map/convert_element_type | solution.py:73
  96.5 0.0 reduce-scatter.5.cloned.1.call-start
  96.6 15.9 %all-gather.6.cloned.1.call-done = bf16[4,2,524288]{2,1,0:T(2,128)(2,1)} async-done(((bf16[4,2,16384]{2,1,0:T(2,128)(2,1)}), bf16[4,2,524288]{2,1,0:T(2,128)(2,1)}) %all-gather.6.cloned.1.call-update) | async-done | bytes 8388624 | tf_op jit(solution)/shard_map/all_gather | solution.py:43
  112.5 101.0 %all_to_all.20 = bf16[4,2,524288]{2,1,0:T(2,128)(2,1)} all-to-all(bf16[4,2,524288]{2,1,0:T(2,128)(2,1)} %all-gather.6.cloned.1.call-done), channel_id=1, replica_groups=mesh['grp'=4,'fsdp'=32] {'grp'}, dimensions={0} | all-to-all | bytes 16777216 | tf_op jit(solution)/shard_map/all_to_all | solution.py:47
  213.5 11.4 %reshape_reshape.6 = bf16[512,8192]{1,0:T(8,128)(2,1)} reshape(bf16[4,2,524288]{2,1,0:T(2,128)(2,1)} %all_to_all.20) | data formatting | bytes 16777216 | tf_op jit(solution)/shard_map/reshape;reshape | solution.py:52
  225.0 6.9 %fusion.4 = bf16[256,512]{0,1:T(8,128)(2,1)S(1)} fusion(f32[256,512]{0,1:T(8,128)S(1)} %bitcast.38, bf16[512,8192]{1,0:T(8,128)(2,1)} %reshape_reshape.6, bf16[256,8192]{1,0:T(8,128)(2,1)} %param.7), kind=kOutput, calls=%fused_computation.15 | convolution fusion | flops 2147745792 | bytes 13369344 | tf_op jit(solution)/shard_map/dot_general | solution.py:12
  231.9 0.4 multiply_convert_fusion.1
  232.3 1.5 copy.15
  233.9 0.0 all-gather.4.cloned.1.call-start
  234.0 0.5 all-gather.4.cloned.1.call-update
  234.5 0.0 reduce-scatter.3.cloned.1.call-done
  234.5 1.2 copy.14
  235.8 0.9 convert_element_type.53
  236.7 3.4 all-to-all-start.2
  240.1 0.1 eq.35
  240.2 5.4 %all-to-all-done.2 = bf16[4,2,16384]{2,1,0:T(2,128)(2,1)S(1)} async-done(((bf16[4,2,16384]{2,1,0:T(2,128)(2,1)}), bf16[4,2,16384]{2,1,0:T(2,128)(2,1)S(1)}, u32[]{:S(2)}, u32[]{:S(2)}) %all-to-all-start.2) | async-done | bytes 262176 | tf_op jit(solution)/shard_map/all_to_all | solution.py:86
  245.6 0.1 reshape.34
  245.7 3.2 convolution_convert_fusion
  248.9 9.1 %fusion.8 = f32[256,8192]{1,0:T(8,128)} fusion(bf16[256,512]{0,1:T(8,128)(2,1)S(1)} %fusion.5, bf16[512,8192]{1,0:T(8,128)(2,1)} %reshape_reshape.6), kind=kOutput, calls=%fused_computation.29 | convolution fusion | flops 2147483648 | bytes 17039360 | tf_op jit(solution)/shard_map/dot_general | solution.py:66
  258.0 50.0 %reduce-scatter.5.cloned.1.call-done = bf16[8,2,1024]{2,0,1:T(8,128)(2,1)} async-done(((bf16[8,64,1024]{2,0,1:T(8,128)(2,1)}), bf16[8,2,1024]{2,0,1:T(8,128)(2,1)}) %reduce-scatter.5.cloned.1.call-update) | async-done | bytes 32784 | tf_op jit(solution)/shard_map/reduce_scatter | solution.py:78
  308.0 0.8 copy.16
  308.8 0.6 convert_element_type.57
  309.4 4.2 %all-to-all-start.3 = ((bf16[4,2,2048]{2,1,0:T(2,128)(2,1)}), bf16[4,2,2048]{2,1,0:T(2,128)(2,1)S(1)}, u32[]{:S(2)}, u32[]{:S(2)}) async-start(bf16[4,2,2048]{2,1,0:T(2,128)(2,1)} %convert_element_type.57), calls=%async_computation.5 | async-start | bytes 65536 | tf_op jit(solution)/shard_map/all_to_all | solution.py:93
  313.6 0.5 convolution_multiply_fusion
  314.0 3.8 all-to-all-done.3
  317.9 1.1 convolution_convert_fusion.1
  319.0 65.0 %all-gather.4.cloned.1.call-done = bf16[8192,1024]{1,0:T(8,128)(2,1)} async-done(((bf16[256,1024]{1,0:T(8,128)(2,1)}), bf16[8192,1024]{1,0:T(8,128)(2,1)}) %all-gather.4.cloned.1.call-update) | async-done | bytes 16777232 | tf_op jit(solution)/shard_map/all_gather | solution.py:59
  383.9 12.3 %fusion.1 = bf16[256,1024]{1,0:T(8,128)(2,1)} fusion(f32[256,1024]{1,0:T(8,128)S(1)} %convolution_multiply_fusion, bf16[256,8192]{1,0:T(8,128)(2,1)} %param.7, bf16[8192,1024]{1,0:T(8,128)(2,1)} %all-gather.4.cloned.1.call-done), kind=kOutput, calls=%fused_computation.10 | convolution fusion | flops 4295491584 | bytes 22544384 | tf_op jit(solution)/shard_map/dot_general | solution.py:60
  396.3 12.3 %fusion = bf16[256,8192]{1,0:T(8,128)(2,1)} fusion(f32[256,8192]{1,0:T(8,128)} %fusion.8, bf16[256,1024]{1,0:T(8,128)(2,1)S(1)} %copy-done, bf16[8192,1024]{1,0:T(8,128)(2,1)} %all-gather.4.cloned.1.call-done), kind=kOutput, calls=%fused_computation.5 | convolution fusion | flops 4299161600 | bytes 29884416 | tf_op jit(solution)/shard_map/dot_general | solution.py:12
  (11 shorter events, 0.2 us)
Async XLA Ops:
  7.2 69.8 %copy-start = (bf16[256,1024]{1,0:T(8,128)(2,1)S(1)}, bf16[256,1024]{1,0:T(8,128)(2,1)}, u32[]{:S(2)}) copy-start(bf16[256,1024]{1,0:T(8,128)(2,1)} %param.13) | copy-start | bytes 1572868
  7.2 50.1 %all-gather.8.cloned.1.call-start = ((), (), s32[]{:S(2)}) async-start(), calls=%async_computation.8 | async-start | bytes 1081344 | tf_op jit(solution)/shard_map/all_gather | solution.py:44
  10.6 101.8 %all-gather.6.cloned.1.call-start = ((), (), s32[]{:S(2)}) async-start(), calls=%async_computation.7 | async-start | bytes 8650752 | tf_op jit(solution)/shard_map/all_gather | solution.py:43
  57.3 18.8 %all-to-all-start.1 = ((bf16[4,2,65536]{2,1,0:T(2,128)(2,1)}), bf16[4,2,65536]{2,1,0:T(2,128)(2,1)S(1)}, u32[]{:S(2)}, u32[]{:S(2)}) async-start(bf16[4,2,65536]{2,1,0:T(2,128)(2,1)} %all-gather.8.cloned.1.call-done), calls=%async_computation.1 | async-start | bytes 2097152 | tf_op jit(solution)/shard_map/all_to_all | solution.py:48
  61.4 173.1 %reduce-scatter.3.cloned.1.call-start = ((), (), s32[]{:S(2)}) async-start(), calls=%async_computation.9 | async-start | bytes 8650752 | tf_op jit(solution)/shard_map/reduce_scatter | solution.py:72
  96.5 211.4 %reduce-scatter.5.cloned.1.call-start = ((), (), s32[]{:S(2)}) async-start(), calls=%async_computation.10 | async-start | bytes 1081344 | tf_op jit(solution)/shard_map/reduce_scatter | solution.py:78
  233.9 150.0 %all-gather.4.cloned.1.call-start = ((), (), s32[]{:S(2)}) async-start(), calls=%async_computation.6 | async-start | bytes 17301504 | tf_op jit(solution)/shard_map/all_gather | solution.py:59
  236.7 8.9 %all-to-all-start.2 = ((bf16[4,2,16384]{2,1,0:T(2,128)(2,1)}), bf16[4,2,16384]{2,1,0:T(2,128)(2,1)S(1)}, u32[]{:S(2)}, u32[]{:S(2)}) async-start(bf16[4,2,16384]{2,1,0:T(2,128)(2,1)} %convert_element_type.53), calls=%async_computation.3 | async-start | bytes 524288 | tf_op jit(solution)/shard_map/all_to_all | solution.py:86
  309.4 8.5 %all-to-all-start.3 = ((bf16[4,2,2048]{2,1,0:T(2,128)(2,1)}), bf16[4,2,2048]{2,1,0:T(2,128)(2,1)S(1)}, u32[]{:S(2)}, u32[]{:S(2)}) async-start(bf16[4,2,2048]{2,1,0:T(2,128)(2,1)} %convert_element_type.57), calls=%async_computation.5 | async-start | bytes 65536 | tf_op jit(solution)/shard_map/all_to_all | solution.py:93
Sparse Core Ops, SparseCore 0:
  10.8 46.4 all-gather.7
  60.2 52.2 all-gather.5
  116.2 90.4 reduce-scatter.2
  234.0 73.8 reduce-scatter.4
  310.1 73.7 all-gather.3
where the time goes:
time: 416 us; the launch traced here: 415 us
  waiting for transfers between devices  196 us (47%)
  blocking collectives  101 us (24%)
  matrix products  54.2 us (13%)
  local copies, waits for them, and re-layouts  35.2 us (8%)
  between operations  13.9 us (3%)
  starting transfers between devices  11.9 us (3%)
    all_to_all x1, blocking collectives, local(): lax.all_to_all(whole_a, 'grp', split_axis=0, concat_axis=0, tiled=True)  101 us
    all_gather x1, waiting for transfers between devices, local(): full_weight = lax.all_gather(weight, 'fsdp', axis=0, tiled=True)  65 us
    reduce_scatter x1, waiting for transfers between devices, local(): lax.psum_scatter(term_b.reshape(slot_count, rank_size, out_width).astype(...  50 us
    all_gather x1, waiting for transfers between devices, local(): lax.all_gather(chosen_b, 'fsdp', axis=2, tiled=True)  41.7 us
    dot_general x3, matrix products, contract_last(): lax.dot_general(left, right, (((1,), (1,)), ((), ())), preferred_element_...  19.8 us
    all_gather x1, waiting for transfers between devices, local(): lax.all_gather(chosen_a, 'fsdp', axis=2, tiled=True)  15.9 us
    all_to_all x1, waiting for transfers between devices, local(): lax.all_to_all(whole_b, 'grp', split_axis=0, concat_axis=0, tiled=True)  13.2 us
    dot_general x1, matrix products, local(): base_out = jnp.dot(tokens, full_weight, preferred_element_type=jnp.float32)  12.3 us
  transfers between devices with their start and end apart: 8, of which 7 were waited for; matrix products, arithmetic and copies ran while one was open for 16% of the time, Pallas kernels for 0%

commit v1 on v0

v1 whole, which is shorter than its diff:
```python
import math

import jax
import jax.numpy as jnp
from jax import lax
from jax.sharding import PartitionSpec as P

SCALE = 2.0


def contract_last(left, right):
    return lax.dot_general(
        left, right, (((1,), (1,)), ((), ())), preferred_element_type=jnp.float32
    )


def contract_first(left, right):
    return lax.dot_general(
        left, right, (((0,), (0,)), ((), ())), preferred_element_type=jnp.float32
    )


def local(tokens, tenant, slot_table, weight, adapter_a, adapter_b, cotangent):
    row_count, width = tokens.shape
    out_width = weight.shape[1]
    group_count = lax.axis_size("grp")
    part_count = lax.axis_size("fsdp")
    group_id = lax.axis_index("grp")
    slot_count = slot_table.shape[1]
    per_owner = slot_count // group_count
    owned_count = adapter_a.shape[0]
    width_a = adapter_a.shape[1]
    width_b = adapter_b.shape[1]
    own_ranks = width_a // width
    own_slots = lax.dynamic_index_in_dim(slot_table, group_id, 0, keepdims=False)
    wanted = (
        lax.dynamic_slice_in_dim(slot_table, group_id * per_owner, per_owner, 1)
        - group_id * owned_count
    )
    hits = (
        wanted.reshape(-1, 1) == jnp.arange(owned_count, dtype=jnp.int32)[None, :]
    ).astype(jnp.bfloat16)
    chosen_b = jnp.dot(hits, adapter_b, preferred_element_type=jnp.float32).astype(jnp.bfloat16)
    chosen_a = jnp.dot(hits, adapter_a, preferred_element_type=jnp.float32).astype(jnp.bfloat16)

    def exchange(chosen):
        return lax.all_to_all(
            chosen.reshape(group_count, per_owner, -1), "grp", 0, 0, tiled=True
        )

    landed_b = exchange(chosen_b).reshape(slot_count * own_ranks, out_width)
    landed_a = exchange(chosen_a).reshape(slot_count * own_ranks, width)
    stack_b = lax.all_gather(landed_b, "fsdp", axis=0, tiled=True)
    stack_a = lax.all_gather(landed_a, "fsdp", axis=0, tiled=True)
    full_weight = lax.all_gather(weight, "fsdp", axis=0, tiled=True)
    row_mask = jnp.tile(
        jnp.repeat((tenant[:, None] == own_slots[None, :]).astype(jnp.float32), own_ranks, axis=1),
        (1, part_count),
    )
    row_scale = 1.0 / math.sqrt(row_count * part_count)
    back_proj = (SCALE * row_mask * contract_last(cotangent, stack_b)).astype(jnp.bfloat16)
    term_a = (contract_first(back_proj, tokens) * row_scale).astype(jnp.bfloat16)
    summed_a = lax.psum_scatter(term_a, "fsdp", scatter_dimension=0, tiled=True)
    low_proj = (contract_last(tokens, stack_a) * row_mask).astype(jnp.bfloat16)
    term_b = (contract_first(low_proj, cotangent) * (SCALE * row_scale)).astype(jnp.bfloat16)
    summed_b = lax.psum_scatter(term_b, "fsdp", scatter_dimension=0, tiled=True)
    base_out = jnp.dot(tokens, full_weight, preferred_element_type=jnp.float32)
    output = (
        base_out + SCALE * jnp.dot(low_proj, stack_b, preferred_element_type=jnp.float32)
    ).astype(jnp.bfloat16)
    token_grad = (
        contract_last(cotangent, full_weight)
        + jnp.dot(back_proj, stack_a, preferred_element_type=jnp.float32)
    ).astype(jnp.bfloat16)
    home_a = exchange(summed_a.reshape(slot_count, width_a)).reshape(slot_count, width_a)
    home_b = exchange(summed_b.reshape(slot_count, width_b)).reshape(slot_count, width_b)
    grad_a = contract_first(hits, home_a).astype(jnp.bfloat16)
    grad_b = contract_first(hits, home_b).astype(jnp.bfloat16)
    return (output, token_grad, grad_a, grad_b)


def solution(mesh):
    return jax.shard_map(
        local,
        mesh=mesh,
        in_specs=(
            P(("grp", "fsdp"), None),
            P(("grp", "fsdp")),
            P(),
            P("fsdp", None),
            P("grp", "fsdp"),
            P("grp", "fsdp"),
            P(("grp", "fsdp"), None),
        ),
        out_specs=(
            P(("grp", "fsdp"), None),
            P(("grp", "fsdp"), None),
            P("grp", "fsdp"),
            P("grp", "fsdp"),
        ),
        check_vma=False,
    )
```

time: 416 us -> 402 us (0.966)
  waiting for transfers between devices: 196 us -> 288 us
  blocking collectives: 101 us -> 27.3 us
  local copies, waits for them, and re-layouts: 35.2 us -> 5.28 us
  starting transfers between devices: 11.9 us -> 4.35 us
  matrix products: 54.2 us -> 60.9 us
    reduce_scatter x2, waiting for transfers between devices: 50 us -> 143 us  [the longest x1 84.8 us: local(): summed_a = lax.psum_scatter(term_a, 'fsdp', scatter_dimension=0, tiled=True)]
    all_to_all x1 -> x3, blocking collectives: 101 us -> 27.3 us  [exchange(): lax.all_to_all(chosen.reshape(group_count, per_owner, -1), 'grp', 0, 0, t...]
    all_to_all x3 -> x1, waiting for transfers between devices: 22.4 us -> 3.84 us  [exchange(): lax.all_to_all(chosen.reshape(group_count, per_owner, -1), 'grp', 0, 0, t...]
    all_gather x2, waiting for transfers between devices: 57.6 us -> 76.1 us  [the longest x1 45.4 us: local(): stack_a = lax.all_gather(landed_a, 'fsdp', axis=0, tiled=True)]
    convert_element_type x4 -> x0, local copies, waits for them, and re-layouts: 14.3 us -> none  [the longest x1 11.2 us: local(): term_a.reshape(slot_count, rank_size, width).astype(jnp.bfloat16)]
    another operation x2 -> x4, local copies, waits for them, and re-layouts: 12.3 us -> 2.62 us  [the longest x2 2.55 us: exchange(): chosen.reshape(group_count, per_owner, -1)]
    all_to_all x3 -> x1, starting transfers between devices: 11.7 us -> 4.14 us  [exchange(): lax.all_to_all(chosen.reshape(group_count, per_owner, -1), 'grp', 0, 0, t...]
    gather x4 -> x0, local copies, waits for them, and re-layouts: 5.59 us -> none  [the longest x2 3.85 us: local(): chosen_a = jnp.take(adapter_a, wanted, axis=0)]
  transfers between devices with their start and end apart: 8 -> 6, of which waited for: 7 -> 6; matrix products, arithmetic and copies ran while one was open for 16% -> 10% of each run, Pallas kernels for 0% -> 0%
where the time goes in v1:
time: 402 us; the launch traced here: 401 us
  waiting for transfers between devices  288 us (72%)
  matrix products  60.9 us (15%)
  blocking collectives  27.3 us (7%)
  between operations  13.9 us (3%)
  local copies, waits for them, and re-layouts  5.28 us (1%)
  starting transfers between devices  4.35 us (1%)
    reduce_scatter x1, waiting for transfers between devices, local(): summed_a = lax.psum_scatter(term_a, 'fsdp', scatter_dimension=0, tiled=True)  84.8 us
    all_gather x1, waiting for transfers between devices, local(): full_weight = lax.all_gather(weight, 'fsdp', axis=0, tiled=True)  64.9 us
    reduce_scatter x1, waiting for transfers between devices, local(): summed_b = lax.psum_scatter(term_b, 'fsdp', scatter_dimension=0, tiled=True)  58 us
    all_gather x1, waiting for transfers between devices, local(): stack_a = lax.all_gather(landed_a, 'fsdp', axis=0, tiled=True)  45.4 us
    all_gather x1, waiting for transfers between devices, local(): stack_b = lax.all_gather(landed_b, 'fsdp', axis=0, tiled=True)  30.7 us
    all_to_all x3, blocking collectives, exchange(): lax.all_to_all(chosen.reshape(group_count, per_owner, -1), 'grp', 0, 0, t...  27.3 us
    dot_general x3, matrix products, contract_last(): lax.dot_general(left, right, (((1,), (1,)), ((), ())), preferred_element_...  21 us
    dot_general x4, matrix products, contract_first(): lax.dot_general(left, right, (((0,), (0,)), ((), ())), preferred_element_...  13.8 us
  transfers between devices with their start and end apart: 6, of which 6 were waited for; matrix products, arithmetic and copies ran while one was open for 10% of the time, Pallas kernels for 0%

profile of v1, /device:TPU:1, one launch (start us, length us, event | category | flops | bytes accessed | tf_op | source)
XLA Modules:
  0.0 401.4 jit_solution(5595037769437122550)
XLA Ops:
  7.2 0.0 copy-start
  7.2 0.0 all-gather.8.cloned.1.call-start
  7.2 0.8 dynamic-slice_subtract_fusion
  8.0 0.1 eq.30
  8.1 1.3 convolution_convert_fusion.3
  9.4 10.0 %all_to_all.20 = bf16[4,2,2048]{2,1,0:T(2,128)(2,1)S(1)} all-to-all(bf16[4,2,2048]{2,1,0:T(2,128)(2,1)S(1)} %reshape.35), channel_id=1, replica_groups=mesh['grp'=4,'fsdp'=32] {'grp'}, dimensions={0} | all-to-all | bytes 65536 | tf_op jit(solution)/shard_map/all_to_all | solution.py:47
  19.4 0.6 reshape.36
  20.0 0.0 all-gather.8.cloned.1.call-update
  20.1 0.0 all-gather.6.cloned.1.call-start
  20.1 2.9 convolution_convert_fusion.1
  23.0 0.2 reshape.33
  23.2 7.9 %all_to_all.21 = bf16[4,2,16384]{2,1,0:T(2,128)(2,1)S(1)} all-to-all(bf16[4,2,16384]{2,1,0:T(2,128)(2,1)S(1)} %reshape.33), channel_id=1, replica_groups=mesh['grp'=4,'fsdp'=32] {'grp'}, dimensions={0} | all-to-all | bytes 524288 | tf_op jit(solution)/shard_map/all_to_all | solution.py:47
  31.1 0.9 reshape.34
  32.0 0.0 all-gather.6.cloned.1.call-update
  32.0 0.0 reduce-scatter.3.cloned.1.call-start
  32.1 0.7 dynamic-slice_bitcast_fusion
  32.7 0.7 compare_convert_fusion
  33.6 30.7 %all-gather.8.cloned.1.call-done = bf16[512,1024]{1,0:T(8,128)(2,1)} async-done(((bf16[16,1024]{1,0:T(8,128)(2,1)}), bf16[512,1024]{1,0:T(8,128)(2,1)}) %all-gather.8.cloned.1.call-update) | async-done | bytes 1048592 | tf_op jit(solution)/shard_map/all_gather | solution.py:53
  64.2 0.0 copy-done
  64.2 1.7 fusion.5
  65.9 7.8 %multiply_convert_fusion = bf16[512,8192]{1,0:T(8,128)(2,1)} fusion(bf16[256,512]{0,1:T(8,128)(2,1)S(1)} %fusion.5, bf16[256,8192]{1,0:T(8,128)(2,1)} %param.7), kind=kOutput, calls=%fused_computation.2 | convolution fusion | flops 2155872256 | bytes 12845056 | tf_op jit(solution)/shard_map/dot_general | solution.py:18
  73.7 0.0 reduce-scatter.3.cloned.1.call-update
  73.8 0.0 reduce-scatter.5.cloned.1.call-start
  73.8 45.4 %all-gather.6.cloned.1.call-done = bf16[512,8192]{1,0:T(8,128)(2,1)} async-done(((bf16[16,8192]{1,0:T(8,128)(2,1)}), bf16[512,8192]{1,0:T(8,128)(2,1)}) %all-gather.6.cloned.1.call-update) | async-done | bytes 8388624 | tf_op jit(solution)/shard_map/all_gather | solution.py:54
  119.3 6.9 %fusion.4 = bf16[256,512]{0,1:T(8,128)(2,1)S(1)} fusion(f32[256,512]{0,1:T(8,128)S(1)} %bitcast.38, bf16[512,8192]{1,0:T(8,128)(2,1)} %all-gather.6.cloned.1.call-done, bf16[256,8192]{1,0:T(8,128)(2,1)} %param.7), kind=kOutput, calls=%fused_computation.15 | convolution fusion | flops 2147745792 | bytes 13369344 | tf_op jit(solution)/shard_map/dot_general | solution.py:12
  126.2 1.4 multiply_convert_fusion.1
  127.6 0.0 reduce-scatter.5.cloned.1.call-update
  127.7 0.0 all-gather.4.cloned.1.call-start
  127.7 0.5 all-gather.4.cloned.1.call-update
  128.2 84.8 %reduce-scatter.3.cloned.1.call-done = bf16[16,8192]{1,0:T(8,128)(2,1)} async-done(((bf16[512,8192]{1,0:T(8,128)(2,1)}), bf16[16,8192]{1,0:T(8,128)(2,1)}) %reduce-scatter.3.cloned.1.call-update) | async-done | bytes 262160 | tf_op jit(solution)/shard_map/reduce_scatter | solution.py:63
  213.1 1.2 reshape_reshape.6
  214.2 9.5 %all_to_all.22 = bf16[4,2,16384]{2,1,0:T(2,128)(2,1)S(1)} all-to-all(bf16[4,2,16384]{2,1,0:T(2,128)(2,1)S(1)} %reshape_reshape.6), channel_id=1, replica_groups=mesh['grp'=4,'fsdp'=32] {'grp'}, dimensions={0} | all-to-all | bytes 524288 | tf_op jit(solution)/shard_map/all_to_all | solution.py:47
  223.7 0.1 reshape.37
  223.8 3.4 convolution_convert_fusion
  227.2 0.0 copy-start.1
  227.2 9.2 %fusion.10 = f32[256,8192]{1,0:T(8,128)} fusion(bf16[256,512]{0,1:T(8,128)(2,1)S(1)} %fusion.5, bf16[512,8192]{1,0:T(8,128)(2,1)} %all-gather.6.cloned.1.call-done), kind=kOutput, calls=%fused_computation.26 | convolution fusion | flops 2147483648 | bytes 17039360 | tf_op jit(solution)/shard_map/dot_general | solution.py:73
  236.3 58.0 %reduce-scatter.5.cloned.1.call-done = bf16[16,1024]{1,0:T(8,128)(2,1)} async-done(((bf16[512,1024]{1,0:T(8,128)(2,1)}), bf16[16,1024]{1,0:T(8,128)(2,1)}) %reduce-scatter.5.cloned.1.call-update) | async-done | bytes 32784 | tf_op jit(solution)/shard_map/reduce_scatter | solution.py:66
  294.3 1.4 reshape_reshape.7
  295.7 4.1 %all-to-all-start.3 = ((bf16[4,2,2048]{2,1,0:T(2,128)(2,1)}), bf16[4,2,2048]{2,1,0:T(2,128)(2,1)S(1)}, u32[]{:S(2)}, u32[]{:S(2)}) async-start(bf16[4,2,2048]{2,1,0:T(2,128)(2,1)} %reshape_reshape.7), calls=%async_computation.5 | async-start | bytes 65536 | tf_op jit(solution)/shard_map/all_to_all | solution.py:47
  299.8 0.0 copy-done.1
  299.8 0.5 convolution_multiply_fusion
  300.3 3.8 all-to-all-done.3
  304.2 1.2 convolution_convert_fusion.2
  305.4 64.9 %all-gather.4.cloned.1.call-done = bf16[8192,1024]{1,0:T(8,128)(2,1)} async-done(((bf16[256,1024]{1,0:T(8,128)(2,1)}), bf16[8192,1024]{1,0:T(8,128)(2,1)}) %all-gather.4.cloned.1.call-update) | async-done | bytes 16777232 | tf_op jit(solution)/shard_map/all_gather | solution.py:55
  370.2 12.3 %fusion.1 = bf16[256,1024]{1,0:T(8,128)(2,1)} fusion(f32[256,1024]{1,0:T(8,128)S(1)} %convolution_multiply_fusion, bf16[256,8192]{1,0:T(8,128)(2,1)} %param.7, bf16[8192,1024]{1,0:T(8,128)(2,1)} %all-gather.4.cloned.1.call-done), kind=kOutput, calls=%fused_computation.10 | convolution fusion | flops 4295491584 | bytes 22544384 | tf_op jit(solution)/shard_map/dot_general | solution.py:67
  382.6 12.3 %fusion = bf16[256,8192]{1,0:T(8,128)(2,1)} fusion(f32[256,8192]{1,0:T(8,128)} %fusion.10, bf16[256,1024]{1,0:T(8,128)(2,1)S(1)} %copy-done, bf16[8192,1024]{1,0:T(8,128)(2,1)} %all-gather.4.cloned.1.call-done), kind=kOutput, calls=%fused_computation.4 | convolution fusion | flops 4299161600 | bytes 29884416 | tf_op jit(solution)/shard_map/dot_general | solution.py:12
  (6 shorter events, 0.2 us)
Async XLA Ops:
  7.2 57.1 %copy-start = (bf16[256,1024]{1,0:T(8,128)(2,1)S(1)}, bf16[256,1024]{1,0:T(8,128)(2,1)}, u32[]{:S(2)}) copy-start(bf16[256,1024]{1,0:T(8,128)(2,1)} %param.13) | copy-start | bytes 1572868
  7.2 57.1 %all-gather.8.cloned.1.call-start = ((), (), s32[]{:S(2)}) async-start(), calls=%async_computation.8 | async-start | bytes 1081344 | tf_op jit(solution)/shard_map/all_gather | solution.py:53
  20.1 99.2 %all-gather.6.cloned.1.call-start = ((), (), s32[]{:S(2)}) async-start(), calls=%async_computation.7 | async-start | bytes 8650752 | tf_op jit(solution)/shard_map/all_gather | solution.py:54
  32.0 181.1 %reduce-scatter.3.cloned.1.call-start = ((), (), s32[]{:S(2)}) async-start(), calls=%async_computation.9 | async-start | bytes 8650752 | tf_op jit(solution)/shard_map/reduce_scatter | solution.py:63
  73.8 220.5 %reduce-scatter.5.cloned.1.call-start = ((), (), s32[]{:S(2)}) async-start(), calls=%async_computation.10 | async-start | bytes 1081344 | tf_op jit(solution)/shard_map/reduce_scatter | solution.py:66
  127.7 242.6 %all-gather.4.cloned.1.call-start = ((), (), s32[]{:S(2)}) async-start(), calls=%async_computation.6 | async-start | bytes 17301504 | tf_op jit(solution)/shard_map/all_gather | solution.py:55
  227.2 72.7 %copy-start.1 = (bf16[512,1024]{1,0:T(8,128)(2,1)S(1)}, bf16[512,1024]{1,0:T(8,128)(2,1)}, u32[]{:S(2)}) copy-start(bf16[512,1024]{1,0:T(8,128)(2,1)} %all-gather.8.cloned.1.call-done) | copy-start | bytes 3145732
  295.7 8.4 %all-to-all-start.3 = ((bf16[4,2,2048]{2,1,0:T(2,128)(2,1)}), bf16[4,2,2048]{2,1,0:T(2,128)(2,1)S(1)}, u32[]{:S(2)}, u32[]{:S(2)}) async-start(bf16[4,2,2048]{2,1,0:T(2,128)(2,1)} %reshape_reshape.7), calls=%async_computation.5 | async-start | bytes 65536 | tf_op jit(solution)/shard_map/all_to_all | solution.py:47
Sparse Core Ops, SparseCore 0:
  20.2 44.0 all-gather.7
  67.1 52.0 all-gather.5
  122.9 90.0 reduce-scatter.2
  217.4 76.8 reduce-scatter.4
  296.4 73.7 all-gather.3

commit v2 on v1

v2 whole, which is shorter than its diff:
```python
import math

import jax
import jax.numpy as jnp
from jax import lax
from jax.experimental import pallas as pl
from jax.experimental.pallas import tpu as pltpu
from jax.sharding import PartitionSpec as P

SCALE = 2.0
RING = 4
MESSAGES = 200
MESH = pl.DeviceIdType.MESH
ALL = slice(None)
BF16 = jnp.bfloat16
F32 = jnp.float32


def mod(value):
    return lax.rem(value + RING, RING)


def mm(left, right):
    return jnp.dot(left, right, preferred_element_type=F32)


def mm_last(left, right):
    return lax.dot_general(left, right, (((1,), (1,)), ((), ())), preferred_element_type=F32)


def mm_first(left, right):
    return lax.dot_general(left, right, (((0,), (0,)), ((), ())), preferred_element_type=F32)


class Net:
    def __init__(self, send_sems, recv_sems):
        self.z = lax.axis_index("grp")
        part = lax.axis_index("fsdp")
        self.c = lax.rem(part, 2)
        self.y = lax.rem(part // 2, RING)
        self.x = part // (2 * RING)
        self.send_sems, self.recv_sems, self.started = send_sems, recv_sems, []

    def at(self, dx=0, dy=0, dz=0, dc=0):
        x, y, z = mod(self.x + dx), mod(self.y + dy), mod(self.z + dz)
        c = lax.rem(self.c + dc, 2)
        return (z, (x * RING + y) * 2 + c)

    def plane(self, axis, step):
        return self.at(dx=step) if axis == 0 else self.at(dy=step)

    def send(self, source, target, device):
        k = len(self.started)
        copy = pltpu.make_async_remote_copy(
            src_ref=source,
            dst_ref=target,
            send_sem=self.send_sems.at[k],
            recv_sem=self.recv_sems.at[k],
            device_id=device,
            device_id_type=MESH,
        )
        copy.start()
        self.started.append(copy)
        return copy

    def sibling(self, ref):
        return self.send(ref, ref, self.at(dc=1))


class Gather:
    def __init__(self, net, ref, width, rows=ALL, to_sibling=True):
        self.net, self.buffer, self.quarter, self.rows = net, ref, width // 4, rows
        self.to_sibling = to_sibling
        self.near, self.far, self.line, self.rest, self.passed = {}, {}, {}, {}, []

    def ref(self, half, p, s, part, count):
        x, y = (p, s) if half == 0 else (s, p)
        cols = pl.ds((half * 2 + part) * self.quarter, count * self.quarter)
        return self.buffer.at[self.net.c, x, y, self.rows, cols]

    def place(self, half):
        return (self.net.x, self.net.y) if half == 0 else (self.net.y, self.net.x)

    def move(self, ref, axis, step):
        return self.net.send(ref, ref, self.net.plane(axis, step))

    def hand(self, ref):
        if self.to_sibling:
            self.passed.append(self.net.sibling(ref))

    def s1(self):
        for half in (0, 1):
            p, s = self.place(half)
            own = self.ref(half, p, s, 0, 2)
            self.near[half] = self.move(own, half, 1), self.move(own, half, -1)

    def s2(self):
        for half in (0, 1):
            p, s = self.place(half)
            plus, minus = self.near[half]
            plus.wait_recv()
            one = self.move(self.ref(half, mod(p - 1), s, 0, 1), half, 1)
            minus.wait_recv()
            two = self.move(self.ref(half, mod(p + 1), s, 1, 1), half, -1)
            self.far[half] = one, two

    def s3(self):
        for half in (0, 1):
            _, s = self.place(half)
            for copy in self.far[half]:
                copy.wait_recv()
            own = self.ref(half, ALL, s, 0, 2)
            self.line[half] = self.move(own, 1 - half, 1), self.move(own, 1 - half, -1)
            self.hand(own)

    def s4(self):
        for half in (0, 1):
            _, s = self.place(half)
            plus, minus = self.line[half]
            plus.wait_recv()
            one = self.move(self.ref(half, ALL, mod(s - 1), 0, 1), 1 - half, 1)
            minus.wait_recv()
            two = self.move(self.ref(half, ALL, mod(s + 1), 1, 1), 1 - half, -1)
            self.rest[half] = one, two
            self.hand(self.ref(half, ALL, mod(s - 1), 0, 2))
            self.hand(self.ref(half, ALL, mod(s + 1), 0, 2))

    def s5(self):
        for half in (0, 1):
            _, s = self.place(half)
            for copy in self.rest[half]:
                copy.wait_recv()
            self.hand(self.ref(half, ALL, mod(s + 2), 0, 2))

    def finish(self):
        for copy in self.passed:
            copy.wait_recv()


class Scatter:
    def __init__(self, net, terms, line_slots, block_slots, out, width):
        self.net, self.terms, self.out, self.quarter = net, terms, out, width // 4
        self.line_slots, self.block_slots = line_slots, block_slots
        self.copies = {}

    def index(self, half, p, s, part):
        x, y = (p, s) if half == 0 else (s, p)
        return x, y, ALL, pl.ds((half * 2 + part) * self.quarter, self.quarter)

    def place(self, half):
        return (self.net.x, self.net.y) if half == 0 else (self.net.y, self.net.x)

    def first(self, half, slots, axis, block):
        me = self.net.x if axis == 0 else self.net.y
        ahead, behind = self.net.plane(axis, 1), self.net.plane(axis, -1)
        at = self.terms.at
        self.copies[half] = [
            self.net.send(at[block(mod(me + 2), 0)], slots.at[half, 0], ahead),
            self.net.send(at[block(mod(me + 1), 1)], slots.at[half, 1], ahead),
            self.net.send(at[block(mod(me + 2), 1)], slots.at[half, 2], behind),
            self.net.send(at[block(mod(me - 1), 0)], slots.at[half, 3], behind),
        ]

    def add(self, block, slots):
        total = self.terms[block].astype(F32)
        for slot in slots:
            total = total + slot.astype(F32)
        return total

    def s1(self):
        for half in (0, 1):
            self.first(half, self.line_slots, half, lambda p, part, h=half: self.index(h, p, ALL, part))

    def s2(self):
        for half in (0, 1):
            p, _ = self.place(half)
            copies = self.copies[half]
            for k, step, part, slot in ((0, 1, 0, 4), (2, -1, 1, 5)):
                copies[k].wait_recv()
                target = mod(p + step)

                def line(i, _, half=half, k=k, part=part, target=target):
                    block = self.index(half, target, i, part)
                    self.terms[block] = self.add(block, [self.line_slots[half, k, i]]).astype(BF16)
                    return 0

                lax.fori_loop(0, RING, line, 0)
                copies.append(
                    self.net.send(
                        self.terms.at[self.index(half, target, ALL, part)],
                        self.line_slots.at[half, slot],
                        self.net.plane(half, step),
                    )
                )

    def s3(self):
        for half in (0, 1):
            p, _ = self.place(half)
            copies = self.copies[half]
            for k in (1, 3, 4, 5):
                copies[k].wait_recv()
            for part, one, two in ((0, 4, 3), (1, 5, 1)):

                def line(i, _, half=half, part=part, one=one, two=two, p=p):
                    block = self.index(half, p, i, part)
                    slots = [self.line_slots[half, one, i], self.line_slots[half, two, i]]
                    self.terms[block] = self.add(block, slots).astype(BF16)
                    return 0

                lax.fori_loop(0, RING, line, 0)
            self.first(
                half, self.block_slots, 1 - half, lambda s, part, h=half, p=p: self.index(h, p, s, part)
            )

    def s4(self):
        for half in (0, 1):
            p, s = self.place(half)
            copies = self.copies[half]
            for k, step, part, slot in ((0, 1, 0, 4), (2, -1, 1, 5)):
                copies[k].wait_recv()
                block = self.index(half, p, mod(s + step), part)
                self.terms[block] = self.add(block, [self.block_slots[half, k]]).astype(BF16)
                copies.append(
                    self.net.send(
                        self.terms.at[block],
                        self.block_slots.at[half, slot],
                        self.net.plane(1 - half, step),
                    )
                )

    def s5(self):
        for half in (0, 1):
            p, s = self.place(half)
            for k in (1, 3, 4, 5):
                self.copies[half][k].wait_recv()
            for part, one, two in ((0, 4, 3), (1, 5, 1)):
                block = self.index(half, p, s, part)
                slots = [self.block_slots[half, one], self.block_slots[half, two]]
                cols = pl.ds((half * 2 + part) * self.quarter, self.quarter)
                self.out[:, cols] = self.add(block, slots).astype(BF16)


def swap(net, source, landed):
    copies = [
        net.send(source.at[mod(net.z + step)], landed.at[net.z], net.at(dz=step)) for step in (1, 3, 2)
    ]
    landed[net.z] = source[net.z]
    return copies


def fold(q, shape, row_dim):
    row = lax.broadcasted_iota(jnp.int32, shape, row_dim)
    col = lax.broadcasted_iota(jnp.int32, shape, 1 - row_dim)
    same = (row // 4 == col // 16) & (row % 4 == col % 4) & ((col // 4) % 4 == q)
    return jnp.where(same, 1.0, 0.0).astype(BF16)


def kernel(
    picks, mask, tokens, weight, adapter_a, adapter_b, cotangent,
    output, token_grad, home_a, home_b,
    w, sa, sb, tok, cot, tg, ab, t_a, t_b, lx_a, ly_a, lx_b, ly_b, g_a, g_b,
    back, low, back_t, low_t, back_x, low_x, total, pa, pb, ma, mb, ha, hb, na, nb,
    local_sems, send_sems, recv_sems,
):
    net = Net(send_sems, recv_sems)
    x, y, z, c = net.x, net.y, net.z, net.c
    width, out_width = tokens.shape[1], weight.shape[1]
    rows = tokens.shape[0]
    part = width // 4
    part_b = out_width // 4
    row_scale = 1.0 / math.sqrt(rows * 2 * RING * RING)

    loads = [
        pltpu.make_async_copy(adapter_b, ab, local_sems.at[0]),
        pltpu.make_async_copy(weight, w.at[c, x, y], local_sems.at[1]),
        pltpu.make_async_copy(adapter_a.at[:, pl.ds(0, width)], tg.at[pl.ds(0, 128)], local_sems.at[2]),
        pltpu.make_async_copy(adapter_a.at[:, pl.ds(width, width)], tg.at[pl.ds(128, 128)], local_sems.at[3]),
        pltpu.make_async_copy(cotangent, cot.at[c], local_sems.at[4]),
        pltpu.make_async_copy(tokens, tok.at[c], local_sems.at[5]),
    ]
    for load in loads:
        load.start()

    barrier = pltpu.get_barrier_semaphore()
    partners = [net.at(dx=1), net.at(dx=-1), net.at(dy=1), net.at(dy=-1), net.at(dz=1), net.at(dz=-1)]
    partners += [net.at(dz=2), net.at(dc=1)]
    for device in partners:
        pl.semaphore_signal(barrier, inc=1, device_id=device, device_id_type=MESH)
    pl.semaphore_wait(barrier, len(partners))

    own_rows = pl.ds(pl.multiple_of(z * 64, 64), 64)
    gather_w = Gather(net, w, out_width, rows=own_rows, to_sibling=False)
    gather_a = Gather(net, sa, width)
    gather_b = Gather(net, sb, out_width)
    scatter_a = Scatter(net, t_a, lx_a, ly_a, g_a, width)
    scatter_b = Scatter(net, t_b, lx_b, ly_b, g_b, out_width)

    loads[1].wait()
    gather_w.s1()

    loads[0].wait()
    chosen = jnp.zeros((64, part_b), F32)
    for i in range(8):
        chosen += mm(picks[i], ab[:, i * part_b : (i + 1) * part_b])
    pb[...] = chosen.astype(BF16).reshape(pb.shape)
    land_b = swap(net, pb, mb)
    loads[2].wait()
    loads[3].wait()

    def pick_a(k, _):
        cols = pl.ds(pl.multiple_of(k * 512, 512), 512)
        chosen = jnp.zeros((64, 512), F32)
        for i in range(8):
            r, q = i // 4, i % 4
            from_cols = pl.ds(pl.multiple_of(q * part + k * 512, 512), 512)
            chosen += mm(picks[i], tg[r * 128 : (r + 1) * 128, from_cols])
        pa[:, :, cols] = chosen.astype(BF16).reshape(4, 16, 512)
        return 0

    lax.fori_loop(0, part // 512, pick_a, 0)
    land_a = swap(net, pa, ma)

    loads[4].wait()
    loads[5].wait()
    cot_x = net.sibling(cot.at[c])
    tok_x = net.sibling(tok.at[c])

    for copy in land_b:
        copy.wait_recv()
    landed = mb[...].reshape(64, part_b)
    for q in range(4):
        sb[c, x, y, :, q * part_b : (q + 1) * part_b] = mm(fold(q, (16, 64), 0), landed).astype(BF16)
    gather_b.s1()
    gather_w.s2()
    for copy in land_a:
        copy.wait_recv()
    landed = ma[...].reshape(64, part)
    for q in range(4):
        sa[c, x, y, :, q * part : (q + 1) * part] = mm(fold(q, (16, 64), 0), landed).astype(BF16)
    gather_b.s2()
    gather_a.s1()
    gather_b.s3()
    gather_w.s3()
    gather_b.s4()
    gather_a.s2()
    gather_w.s4()
    gather_b.s5()
    gather_w.s5()

    quarter = lambda k, dz, cols=ALL: w.at[
        c, k, :, pl.ds(pl.multiple_of(mod(z + dz) * 64, 64), 64), cols
    ]
    ring, ring_far, passed = {}, {}, {}

    def z_start(k):
        own = quarter(k, 0)
        ring[k] = net.send(own, own, net.at(dz=1)), net.send(own, own, net.at(dz=-1))
        passed[k] = [net.sibling(own)]

    def z_forward(k):
        half = out_width // 2
        plus, minus = ring[k]
        plus.wait_recv()
        one = quarter(k, -1, pl.ds(0, half))
        one = net.send(one, one, net.at(dz=1))
        minus.wait_recv()
        two = quarter(k, 1, pl.ds(half, half))
        two = net.send(two, two, net.at(dz=-1))
        ring_far[k] = one, two
        passed[k] += [net.sibling(quarter(k, -1)), net.sibling(quarter(k, 1))]
        if k + 2 < RING:
            z_start(k + 2)

    def z_finish(k):
        for copy in ring_far[k]:
            copy.wait_recv()
        passed[k].append(net.sibling(quarter(k, 2)))

    z_start(0)
    z_start(1)
    gather_a.s3()
    gather_b.finish()

    stack_b = lambda: sb[...].reshape(512, out_width)
    weights = mask[...].astype(F32)
    found = SCALE * weights * mm_last(cot[c], stack_b())
    back[...] = found.astype(BF16)
    back_t[...] = found.T.astype(BF16).reshape(2, 256, rows)
    swap_back = net.send(back_t.at[1 - c], back_x, net.at(dc=1))
    tok_x.wait_recv()
    cot_x.wait_recv()
    swap_back.wait_recv()

    def terms_a(k, _):
        cols = pl.ds(pl.multiple_of(k * 512, 512), 512)
        found = mm(back_t[c], tok[c, :, cols]) + mm(back_x[...], tok[1 - c, :, cols])
        t_a[:, :, :, cols] = (found * row_scale).astype(BF16).reshape(4, 4, 16, 512)
        return 0

    lax.fori_loop(0, width // 512, terms_a, 0)
    scatter_a.s1()
    gather_a.s4()
    z_forward(0)
    scatter_a.s2()
    gather_a.s5()
    gather_a.finish()

    def low_step(k, acc):
        cols = pl.ds(pl.multiple_of(k * 1024, 1024), 1024)
        return acc + mm_last(tok[c, :, cols], sa[:, :, :, :, cols].reshape(512, 1024))

    found = weights * lax.fori_loop(0, width // 1024, low_step, jnp.zeros((rows, 512), F32))
    low[...] = found.astype(BF16)
    low_t[...] = found.T.astype(BF16).reshape(2, 256, rows)
    swap_low = net.send(low_t.at[1 - c], low_x, net.at(dc=1))
    total[...] = SCALE * mm(low[...], stack_b())
    swap_low.wait_recv()
    found = mm(low_t[c], cot[c]) + mm(low_x[...], cot[1 - c])
    t_b[...] = (found * (SCALE * row_scale)).astype(BF16).reshape(4, 4, 16, out_width)
    scatter_b.s1()
    z_forward(1)
    scatter_a.s3()
    scatter_b.s2()
    scatter_b.s3()
    scatter_a.s4()
    scatter_b.s4()
    z_forward(2)

    stores = []

    def compute(k):
        z_finish(k)
        for copy in passed[k]:
            copy.wait_recv()

        def step(j, _):
            start = pl.multiple_of((k * RING + j) * 512, 512)
            one, two = w[0, k, j], w[1, k, j]
            cols, lo, hi = pl.ds(start, 512), pl.ds(start, 256), pl.ds(start + 256, 256)
            total[...] += mm(tok[c, :, lo], one) + mm(tok[c, :, hi], two)
            from_a = mm(back[...], sa[:, :, :, :, cols].reshape(512, 512))
            tg[:, lo] = (mm_last(cot[c], one) + from_a[:, :256]).astype(BF16)
            tg[:, hi] = (mm_last(cot[c], two) + from_a[:, 256:]).astype(BF16)
            return 0

        lax.fori_loop(0, RING, step, 0)
        cols = pl.ds(k * 4 * 512, 4 * 512)
        store = pltpu.make_async_copy(tg.at[:, cols], token_grad.at[:, cols], local_sems.at[6 + k])
        store.start()
        stores.append(store)

    compute(0)
    scatter_a.s5()
    scatter_b.s5()

    def unfold(source, target, size):
        found = jnp.zeros((64, size), F32)
        for q in range(4):
            found += mm(fold(q, (64, 16), 1), source[:, q * size : (q + 1) * size])
        target[...] = found.astype(BF16).reshape(4, 16, size)

    unfold(g_a, na, part)
    unfold(g_b, nb, part_b)
    back_a = swap(net, na, ha)
    back_b = swap(net, nb, hb)
    z_forward(3)
    compute(1)
    compute(2)
    for copy in back_a + back_b:
        copy.wait_recv()
    home_a[...] = ha[...].reshape(64, part)
    home_b[...] = hb[...].reshape(64, part_b)
    compute(3)
    output[...] = total[...].astype(BF16)
    for store in stores:
        store.wait()
    for copy in net.started:
        copy.wait_send()


def expand_kernel(picks, home_a, home_b, grad_a, grad_b):
    grad_a[...] = mm(picks[0], home_a[...]).astype(BF16)
    grad_b[...] = mm(picks[0], home_b[...]).astype(BF16)


def local(tokens, tenant, slot_table, weight, adapter_a, adapter_b, cotangent):
    rows, width = tokens.shape
    out_width = weight.shape[1]
    groups = lax.axis_size("grp")
    group = lax.axis_index("grp")
    slots = slot_table.shape[1]
    per_owner = slots // groups
    owned = adapter_a.shape[0]
    own_slots = lax.dynamic_index_in_dim(slot_table, group, 0, keepdims=False)
    wanted = lax.dynamic_slice_in_dim(slot_table, group * per_owner, per_owner, 1) - group * owned
    row = jnp.arange(64, dtype=jnp.int32)
    own_id = jnp.repeat(jnp.repeat(wanted, 2, axis=1), 4, axis=0).reshape(64)
    place = (row % 2) * 4 + (row // 4) % 4
    step = jnp.arange(8, dtype=jnp.int32)
    ids = jnp.arange(owned, dtype=jnp.int32)
    picks = (
        (own_id[None, :, None] == ids[None, None, :]) & (place[None, :, None] == step[:, None, None])
    ).astype(BF16)
    picks_t = (
        (own_id[None, None, :] == ids[None, :, None]) & (place[None, None, :] == step[:, None, None])
    ).astype(BF16)
    mask = jnp.tile(jnp.repeat(tenant[:, None] == own_slots[None, :], 2, axis=1), (1, 32)).astype(BF16)

    part, part_b = width // 4, out_width // 4
    vmem, hbm = pl.BlockSpec(memory_space=pltpu.VMEM), pl.BlockSpec(memory_space=pl.ANY)
    buffer = lambda *shape, dtype=BF16: pltpu.VMEM(shape, dtype)
    output, token_grad, home_a, home_b = pl.pallas_call(
        kernel,
        name="exchange_and_multiply",
        out_shape=(
            jax.ShapeDtypeStruct((rows, out_width), BF16),
            jax.ShapeDtypeStruct((rows, width), BF16),
            jax.ShapeDtypeStruct((64, part), BF16),
            jax.ShapeDtypeStruct((64, part_b), BF16),
        ),
        in_specs=[vmem, vmem, hbm, hbm, hbm, hbm, hbm],
        out_specs=(vmem, hbm, vmem, vmem),
        scratch_shapes=[
            buffer(2, 4, 4, 256, out_width),
            buffer(2, 4, 4, 16, width),
            buffer(2, 4, 4, 16, out_width),
            buffer(2, rows, width),
            buffer(2, rows, out_width),
            buffer(rows, width),
            buffer(owned, 2 * out_width),
            buffer(4, 4, 16, width),
            buffer(4, 4, 16, out_width),
            buffer(2, 6, 4, 16, part),
            buffer(2, 6, 16, part),
            buffer(2, 6, 4, 16, part_b),
            buffer(2, 6, 16, part_b),
            buffer(16, width),
            buffer(16, out_width),
            buffer(rows, 512),
            buffer(rows, 512),
            buffer(2, 256, rows),
            buffer(2, 256, rows),
            buffer(256, rows),
            buffer(256, rows),
            buffer(rows, out_width, dtype=F32),
            buffer(4, 16, part),
            buffer(4, 16, part_b),
            buffer(4, 16, part),
            buffer(4, 16, part_b),
            buffer(4, 16, part),
            buffer(4, 16, part_b),
            buffer(4, 16, part),
            buffer(4, 16, part_b),
            pltpu.SemaphoreType.DMA((10,)),
            pltpu.SemaphoreType.DMA((MESSAGES,)),
            pltpu.SemaphoreType.DMA((MESSAGES,)),
        ],
        compiler_params=pltpu.CompilerParams(
            collective_id=0, has_side_effects=True, vmem_limit_bytes=62 * 1024 * 1024
        ),
    )(picks, mask, tokens, weight, adapter_a, adapter_b, cotangent)

    grad_a, grad_b = pl.pallas_call(
        expand_kernel,
        name="expand_grads",
        grid=(8,),
        out_shape=(
            jax.ShapeDtypeStruct(adapter_a.shape, BF16),
            jax.ShapeDtypeStruct(adapter_b.shape, BF16),
        ),
        in_specs=[
            pl.BlockSpec((1, owned, 64), lambda i: (i, 0, 0)),
            pl.BlockSpec((64, part), lambda i: (0, 0)),
            pl.BlockSpec((64, part_b), lambda i: (0, 0)),
        ],
        out_specs=(
            pl.BlockSpec((owned, part), lambda i: (0, i)),
            pl.BlockSpec((owned, part_b), lambda i: (0, i)),
        ),
    )(picks_t, home_a, home_b)
    return (output, token_grad, grad_a, grad_b)


def solution(mesh):
    return jax.shard_map(
        local,
        mesh=mesh,
        in_specs=(
            P(("grp", "fsdp"), None),
            P(("grp", "fsdp")),
            P(),
            P("fsdp", None),
            P("grp", "fsdp"),
            P("grp", "fsdp"),
            P(("grp", "fsdp"), None),
        ),
        out_specs=(
            P(("grp", "fsdp"), None),
            P(("grp", "fsdp"), None),
            P("grp", "fsdp"),
            P("grp", "fsdp"),
        ),
        check_vma=False,
    )
```

time: 402 us -> 135 us (0.34)
  waiting for transfers between devices: 288 us -> 0 us
  Pallas kernels: 0 us -> 122 us
  matrix products: 60.9 us -> 0 us
  blocking collectives: 27.3 us -> 0 us
  between operations: 13.9 us -> 0.68 us
  starting transfers between devices: 4.35 us -> 0 us
    reduce_scatter x2 -> x0, waiting for transfers between devices: 143 us -> none  [the longest x1 84.8 us: local(): summed_a = lax.psum_scatter(term_a, 'fsdp', scatter_dimension=0, tiled=True)]
    all_gather x3 -> x0, waiting for transfers between devices: 141 us -> none  [the longest x1 64.9 us: local(): full_weight = lax.all_gather(weight, 'fsdp', axis=0, tiled=True)]
    pallas_call x0 -> x2, Pallas kernels: none -> 122 us  [the longest x1 116 us: local(): pl.pallas_call(kernel, name='exchange_and_multiply', out_shape=(jax.Shape...]
    dot_general x12 -> x0, matrix products: 60.9 us -> none  [the longest x3 21 us: contract_last(): lax.dot_general(left, right, (((1,), (1,)), ((), ())), preferred_element_...]
    all_to_all x3 -> x0, blocking collectives: 27.3 us -> none  [exchange(): lax.all_to_all(chosen.reshape(group_count, per_owner, -1), 'grp', 0, 0, t...]
    unnamed x4 -> x2, local copies, waits for them, and re-layouts: 0.01 us -> 6.51 us
    all_to_all x1 -> x0, starting transfers between devices: 4.14 us -> none  [exchange(): lax.all_to_all(chosen.reshape(group_count, per_owner, -1), 'grp', 0, 0, t...]
  transfers between devices with their start and end apart: 6 -> 0, of which waited for: 6 -> 0; matrix products, arithmetic and copies ran while one was open for 10% -> 0% of each run, Pallas kernels for 0% -> 0%
where the time goes in v2:
time: 135 us; the launch traced here: 134 us
  Pallas kernels  122 us (90%)
  local copies, waits for them, and re-layouts  8.37 us (6%)
  other arithmetic  3.17 us (2%)
    pallas_call x1, Pallas kernels, local(): pl.pallas_call(kernel, name='exchange_and_multiply', out_shape=(jax.Shape...  116 us
    unnamed x2, local copies, waits for them, and re-layouts  6.51 us
    pallas_call x1, Pallas kernels, local(): pl.pallas_call(expand_kernel, name='expand_grads', grid=(8,), out_shape=(...  6.2 us

profile of v2, /device:TPU:1, one launch (start us, length us, event | category | flops | bytes accessed | tf_op | source)
XLA Modules:
  0.0 134.1 jit_solution(13473306507896106318)
XLA Ops:
  0.6 0.7 dynamic-slice_bitcast_fusion
  1.3 0.8 dynamic-slice_subtract_fusion
  2.1 0.1 copy.13
  2.2 0.1 copy.14
  2.3 0.7 compare_convert_fusion
  3.1 0.1 eq.92
  3.2 0.1 iota_compare_fusion.1
  3.3 0.8 and_convert_fusion.1.picks
  4.1 0.8 and_convert_fusion.picks
  4.9 0.8 copy.15.mask
  5.7 115.7 %exchange_and_multiply.1 = (bf16[256,1024]{1,0:T(8,128)(2,1)}, bf16[256,8192]{1,0:T(8,128)(2,1)}, bf16[64,2048]{1,0:T(8,128)(2,1)}, bf16[64,256]{1,0:T(8,128)(2,1)}) custom-call(bf16[8,64,128]{2,1,0:T(8,128)(2,1)} %and_convert_fusion.1.picks, bf16[256,512]{1,0:T(8,128)(2,1)} %copy.15.mask, bf16[256,8192]{1,0:T(8,128)(2,1)} %tokens.1, ...), custom_call_target="tpu_custom_call" | custom-call | tf_op jit(solution)/shard_map/exchange_and_multiply/pallas_call | solution.py:512
  121.4 6.2 %expand_grads.1 = (bf16[128,16384]{1,0:T(8,128)(2,1)}, bf16[128,2048]{1,0:T(8,128)(2,1)}) custom-call(bf16[8,128,64]{2,1,0:T(8,128)(2,1)} %and_convert_fusion.picks, bf16[64,2048]{1,0:T(8,128)(2,1)} %get-tuple-element.12.home_a, bf16[64,256]{1,0:T(8,128)(2,1)} %get-tuple-element.13.home_b), custom_call_target="tpu_custom_call" | custom-call | tf_op jit(solution)/shard_map/expand_grads/pallas_call | solution.py:563
  127.6 1.9 %copy.18 = bf16[256,1024]{1,0:T(8,128)(2,1)} copy(bf16[256,1024]{1,0:T(8,128)(2,1)} %get-tuple-element.20) | data formatting | bytes 1048576
  129.5 4.6 %copy.19 = bf16[256,8192]{1,0:T(8,128)(2,1)} copy(bf16[256,8192]{1,0:T(8,128)(2,1)} %get-tuple-element.21) | data formatting | bytes 8388608
  (8 shorter events, 0.1 us)

commit v3 on v1

v3 whole, which is shorter than its diff:
```python
import math

import jax
import jax.numpy as jnp
from jax import lax
from jax.experimental import pallas as pl
from jax.experimental.pallas import tpu as pltpu
from jax.sharding import PartitionSpec as P

SCALE = 2.0
RING = 4
SENDS = 64
RECEIVES = 120
ORDER = (
    "w.s1", "d.s1", "swapb", "b.s1", "w.s2", "swapa", "tokx", "d.s2", "b.s2", "w.s3", "a.s1", "b.s3",
    "w.s4", "a.s2", "d.s3", "w.s5", "z0.go", "b.s4", "z1.go", "z2.go", "a.s3", "b.s5", "z0.fw", "d.s4",
    "b.fin", "back", "a.s4", "T0", "T1", "T2", "r0.s1", "z1.fw", "a.s5", "T3", "r1.s1", "a.fin", "d.s5",
    "low0", "z2.fw", "low1", "r0.s2", "z0.en", "z3.go", "tot", "tb", "d.fin", "q.s1", "r1.s2", "z1.en",
    "m0.0", "m1.0", "z4.go", "z2.en", "m0.1", "q.s2", "r0.s3", "m2.0", "r1.s3", "z3.fw", "q.s3", "r0.s4",
    "m1.1", "r1.s4", "q.s4", "z4.fw", "m2.1", "r0.s5", "z3.en", "r1.s5", "q.s5", "unf", "home", "m3.0",
    "z4.en", "m3.1", "m4.0", "m4.1", "homw", "out",
)
SHARED = 64
MESH = pl.DeviceIdType.MESH
ALL = slice(None)
BF16 = jnp.bfloat16
F32 = jnp.float32


def mod(value):
    return lax.rem(value + RING, RING)


def mm(left, right):
    return jnp.dot(left, right, preferred_element_type=F32)


def mm_last(left, right):
    return lax.dot_general(left, right, (((1,), (1,)), ((), ())), preferred_element_type=F32)


def mm_first(left, right):
    return lax.dot_general(left, right, (((0,), (0,)), ((), ())), preferred_element_type=F32)


class Net:
    def __init__(self, send_sems, recv_sems):
        self.z = lax.axis_index("grp")
        part = lax.axis_index("fsdp")
        self.c = lax.rem(part, 2)
        self.y = lax.rem(part // 2, RING)
        self.x = part // (2 * RING)
        self.send_sems, self.recv_sems, self.started, self.places = send_sems, recv_sems, [], 0

    def at(self, dx=0, dy=0, dz=0, dc=0):
        x, y, z = mod(self.x + dx), mod(self.y + dy), mod(self.z + dz)
        c = lax.rem(self.c + dc, 2)
        return (z, (x * RING + y) * 2 + c)

    def plane(self, axis, step):
        return self.at(dx=step) if axis == 0 else self.at(dy=step)

    def place(self):
        self.places += 1
        return self.recv_sems.at[self.places - 1]

    def send(self, source, target, device, sem=None):
        k = len(self.started)
        if k >= SENDS:
            self.started[k - SENDS].wait_send()
        copy = pltpu.make_async_remote_copy(
            src_ref=source,
            dst_ref=target,
            send_sem=self.send_sems.at[k % SENDS],
            recv_sem=self.place() if sem is None else sem,
            device_id=device,
            device_id_type=MESH,
        )
        copy.start()
        self.started.append(copy)
        return copy

    def sibling(self, ref, sem=None):
        return self.send(ref, ref, self.at(dc=1), sem)


def wait_all(region, sem):
    pltpu.make_async_copy(region, region, sem).wait()


class Gather:
    def __init__(self, net, ref, width, rows=ALL, to_sibling=True):
        self.net, self.buffer, self.quarter, self.rows = net, ref, width // 4, rows
        self.near, self.line = {}, {}
        self.far = [net.place(), net.place()]
        self.rest = [net.place(), net.place()]
        self.passed = net.place() if to_sibling else None

    def ref(self, half, p, s, part, count):
        x, y = (p, s) if half == 0 else (s, p)
        cols = pl.ds((half * 2 + part) * self.quarter, count * self.quarter)
        return self.buffer.at[self.net.c, x, y, self.rows, cols]

    def at(self, half):
        return (self.net.x, self.net.y) if half == 0 else (self.net.y, self.net.x)

    def move(self, ref, axis, step, sem=None):
        return self.net.send(ref, ref, self.net.plane(axis, step), sem)

    def hand(self, ref):
        if self.passed is not None:
            self.net.sibling(ref, self.passed)

    def s1(self):
        for half in (0, 1):
            p, s = self.at(half)
            own = self.ref(half, p, s, 0, 2)
            self.near[half] = self.move(own, half, 1), self.move(own, half, -1)

    def s2(self):
        for half in (0, 1):
            p, s = self.at(half)
            plus, minus = self.near[half]
            plus.wait_recv()
            self.move(self.ref(half, mod(p - 1), s, 0, 1), half, 1, self.far[half])
            minus.wait_recv()
            self.move(self.ref(half, mod(p + 1), s, 1, 1), half, -1, self.far[half])

    def s3(self):
        for half in (0, 1):
            p, s = self.at(half)
            wait_all(self.ref(half, mod(p + 2), s, 0, 2), self.far[half])
            own = self.ref(half, ALL, s, 0, 2)
            self.line[half] = self.move(own, 1 - half, 1), self.move(own, 1 - half, -1)
            self.hand(own)

    def s4(self):
        for half in (0, 1):
            _, s = self.at(half)
            plus, minus = self.line[half]
            plus.wait_recv()
            self.move(self.ref(half, ALL, mod(s - 1), 0, 1), 1 - half, 1, self.rest[half])
            minus.wait_recv()
            self.move(self.ref(half, ALL, mod(s + 1), 1, 1), 1 - half, -1, self.rest[half])
            self.hand(self.ref(half, ALL, mod(s - 1), 0, 2))
            self.hand(self.ref(half, ALL, mod(s + 1), 0, 2))

    def s5(self):
        for half in (0, 1):
            _, s = self.at(half)
            last = self.ref(half, ALL, mod(s + 2), 0, 2)
            wait_all(last, self.rest[half])
            self.hand(last)

    def fin(self):
        wait_all(self.buffer.at[1 - self.net.c, :, :, self.rows], self.passed)


class Scatter:
    def __init__(self, net, terms, line_slots, block_slots, out, width, base=0):
        self.net, self.terms, self.out, self.quarter, self.base = net, terms, out, width // 4, base
        self.line_slots, self.block_slots = line_slots, block_slots
        self.sems = [[[net.place() for _ in range(3)] for _ in range(2)] for _ in range(2)]

    def cols(self, half, part):
        return pl.ds(self.base + (half * 2 + part) * self.quarter, self.quarter)

    def index(self, half, p, s, part):
        x, y = (p, s) if half == 0 else (s, p)
        return x, y, ALL, self.cols(half, part)

    def at(self, half):
        return (self.net.x, self.net.y) if half == 0 else (self.net.y, self.net.x)

    def first(self, half, slots, axis, block, sems):
        me = self.net.x if axis == 0 else self.net.y
        ahead, behind = self.net.plane(axis, 1), self.net.plane(axis, -1)
        at, slots, net = self.terms.at, slots.at, self.net
        net.send(at[block(mod(me + 2), 0)], slots[half, 0], ahead, sems[0])
        net.send(at[block(mod(me + 2), 1)], slots[half, 1], behind, sems[1])
        net.send(at[block(mod(me + 1), 1)], slots[half, 2], ahead, sems[2])
        net.send(at[block(mod(me - 1), 0)], slots[half, 3], behind, sems[2])

    def add(self, block, slots):
        total = self.terms[block].astype(F32)
        for slot in slots:
            total = total + slot.astype(F32)
        return total

    def s1(self):
        for half in (0, 1):
            self.first(
                half,
                self.line_slots,
                half,
                lambda p, part, h=half: self.index(h, p, ALL, part),
                self.sems[0][half],
            )

    def s2(self):
        for half in (0, 1):
            p, _ = self.at(half)
            sems = self.sems[0][half]
            for k, step in ((0, 1), (1, -1)):
                wait_all(self.line_slots.at[half, k], sems[k])
                target = mod(p + step)

                def line(i, _, half=half, k=k, target=target):
                    block = self.index(half, target, i, k)
                    self.terms[block] = self.add(block, [self.line_slots[half, k, i]]).astype(BF16)
                    return 0

                lax.fori_loop(0, RING, line, 0)
                self.net.send(
                    self.terms.at[self.index(half, target, ALL, k)],
                    self.line_slots.at[half, 4 + k],
                    self.net.plane(half, step),
                    sems[2],
                )

    def s3(self):
        for half in (0, 1):
            p, _ = self.at(half)
            wait_all(self.line_slots.at[half, pl.ds(2, 4)], self.sems[0][half][2])
            for part in (0, 1):

                def line(i, _, half=half, part=part, p=p):
                    block = self.index(half, p, i, part)
                    slots = [self.line_slots[half, 4 + part, i], self.line_slots[half, 3 - part, i]]
                    self.terms[block] = self.add(block, slots).astype(BF16)
                    return 0

                lax.fori_loop(0, RING, line, 0)
            self.first(
                half,
                self.block_slots,
                1 - half,
                lambda s, part, h=half, p=p: self.index(h, p, s, part),
                self.sems[1][half],
            )

    def s4(self):
        for half in (0, 1):
            p, s = self.at(half)
            sems = self.sems[1][half]
            for k, step in ((0, 1), (1, -1)):
                wait_all(self.block_slots.at[half, k], sems[k])
                block = self.index(half, p, mod(s + step), k)
                self.terms[block] = self.add(block, [self.block_slots[half, k]]).astype(BF16)
                self.net.send(
                    self.terms.at[block],
                    self.block_slots.at[half, 4 + k],
                    self.net.plane(1 - half, step),
                    sems[2],
                )

    def s5(self):
        for half in (0, 1):
            p, s = self.at(half)
            wait_all(self.block_slots.at[half, pl.ds(2, 4)], self.sems[1][half][2])
            for part in (0, 1):
                block = self.index(half, p, s, part)
                slots = [self.block_slots[half, 4 + part], self.block_slots[half, 3 - part]]
                self.out[:, self.cols(half, part)] = self.add(block, slots).astype(BF16)


def swap(net, source, landed):
    sem = net.place()
    for step in (1, 3, 2):
        net.send(source.at[mod(net.z + step)], landed.at[net.z], net.at(dz=step), sem)
    landed[net.z] = source[net.z]
    return landed.at[pl.ds(0, 3)], sem


def fold(q, shape, row_dim):
    row = lax.broadcasted_iota(jnp.int32, shape, row_dim)
    col = lax.broadcasted_iota(jnp.int32, shape, 1 - row_dim)
    same = (row // 4 == col // 16) & (row % 4 == col % 4) & ((col // 4) % 4 == q)
    return jnp.where(same, 1.0, 0.0).astype(BF16)


def wanted(slot_table, z, owned, row):
    found = jnp.zeros(row.shape, jnp.int32)
    for g in range(4):
        for j in range(2):
            here = (row // 16 == g) & ((row // 2) % 2 == j)
            found = found + jnp.where(here, slot_table[g, 2 * z + j] - z * owned, 0)
    return found


def pick(ids, row, adapter, i):
    here = (ids == adapter) & ((row % 2) * 4 + (row // 4) % 4 == i)
    return jnp.where(here, 1.0, 0.0).astype(BF16)


def kernel(
    slot_table, tenant, tokens, weight, adapter_a, adapter_b, cotangent,
    output, token_grad, home_a, home_b,
    w, sa, sb, tok, cot, tg, ab, t_a, t_b, lx_0, ly_0, lx_1, ly_1, lx_b, ly_b, g_a, g_b,
    mask, back, low, back_t, low_t, back_x, low_x, total, pa, pb, ma, mb, ha, hb, na, nb,
    local_sems, send_sems, recv_sems,
):
    net = Net(send_sems, recv_sems)
    x, y, z, c = net.x, net.y, net.z, net.c
    width, out_width = tokens.shape[1], weight.shape[1]
    rows = tokens.shape[0]
    owned = adapter_a.shape[0]
    part = width // 4
    part_b = out_width // 4
    row_scale = 1.0 / math.sqrt(rows * 2 * RING * RING)
    shared, slab = pl.ds(0, SHARED), (256 - SHARED) // RING
    rows_of = lambda dz: pl.ds(pl.multiple_of(SHARED + mod(z + dz) * slab, 16), slab)

    loads = [
        pltpu.make_async_copy(weight.at[rows_of(0)], w.at[c, x, y, rows_of(0)], local_sems.at[0]),
        pltpu.make_async_copy(adapter_b, ab, local_sems.at[1]),
        pltpu.make_async_copy(weight.at[shared], w.at[c, x, y, shared], local_sems.at[2]),
        pltpu.make_async_copy(adapter_a.at[:, pl.ds(0, width)], tg.at[pl.ds(0, 128)], local_sems.at[3]),
        pltpu.make_async_copy(adapter_a.at[:, pl.ds(width, width)], tg.at[pl.ds(128, 128)], local_sems.at[4]),
        pltpu.make_async_copy(cotangent, cot.at[c], local_sems.at[5]),
        pltpu.make_async_copy(tokens, tok.at[c], local_sems.at[6]),
    ]
    for load in loads:
        load.start()

    barrier = pltpu.get_barrier_semaphore()
    partners = [net.at(dx=1), net.at(dx=-1), net.at(dy=1), net.at(dy=-1), net.at(dz=1), net.at(dz=-1)]
    partners += [net.at(dz=2), net.at(dc=1)]
    for device in partners:
        pl.semaphore_signal(barrier, inc=1, device_id=device, device_id_type=MESH)

    steps, state = {}, {}

    def step(name):
        def keep(function):
            steps[name] = function
            return function

        return keep

    def stages(name, collective):
        for stage in ("s1", "s2", "s3", "s4", "s5", "fin"):
            if hasattr(collective, stage):
                steps[name + "." + stage] = getattr(collective, stage)

    gather_w = Gather(net, w, out_width, rows=rows_of(0), to_sibling=False)
    gather_d = Gather(net, w, out_width, rows=shared)
    gather_a = Gather(net, sa, width)
    gather_b = Gather(net, sb, out_width)
    stages("w", gather_w)
    stages("d", gather_d)
    stages("a", gather_a)
    stages("b", gather_b)
    half = width // 2
    stages("r0", Scatter(net, t_a, lx_0, ly_0, g_a, half))
    stages("r1", Scatter(net, t_a, lx_1, ly_1, g_a, half, base=half))
    stages("q", Scatter(net, t_b, lx_b, ly_b, g_b, out_width))

    row = lax.broadcasted_iota(jnp.int32, (64, owned), 0)
    adapter = lax.broadcasted_iota(jnp.int32, (64, owned), 1)
    ids = wanted(slot_table, z, owned, row)
    picks = [pick(ids, row, adapter, i) for i in range(8)]
    slot = lax.broadcasted_iota(jnp.int32, (16, rows), 0) // 2
    slot_ids = jnp.zeros((16, rows), jnp.int32)
    for s in range(8):
        slot_ids = slot_ids + jnp.where(slot == s, slot_table[z, s], 0)
    hit = jnp.where(slot_ids == tenant[...], 1.0, 0.0)
    mask[...] = jnp.concatenate([hit] * 32, axis=0).T
    for load in loads[:3]:
        load.wait()
    chosen = jnp.zeros((64, part_b), F32)
    for i in range(8):
        chosen += mm(picks[i], ab[:, i * part_b : (i + 1) * part_b])
    pb[...] = chosen.astype(BF16).reshape(pb.shape)

    @step("swapb")
    def _():
        state["lb"] = swap(net, pb, mb)

    @step("swapa")
    def _():
        loads[3].wait()
        loads[4].wait()

        def pick_a(k, _):
            cols = pl.ds(pl.multiple_of(k * 512, 512), 512)
            chosen = jnp.zeros((64, 512), F32)
            for i in range(8):
                r, q = i // 4, i % 4
                from_cols = pl.ds(pl.multiple_of(q * part + k * 512, 512), 512)
                chosen += mm(picks[i], tg[r * 128 : (r + 1) * 128, from_cols])
            pa[:, :, cols] = chosen.astype(BF16).reshape(4, 16, 512)
            return 0

        lax.fori_loop(0, part // 512, pick_a, 0)
        state["la"] = swap(net, pa, ma)

    @step("tokx")
    def _():
        loads[5].wait()
        loads[6].wait()
        state["cx"] = net.sibling(cot.at[c])
        state["tx"] = net.sibling(tok.at[c])

    @step("b.s1")
    def _():
        wait_all(*state["lb"])
        landed = mb[...].reshape(64, part_b)
        for q in range(4):
            sb[c, x, y, :, q * part_b : (q + 1) * part_b] = mm(fold(q, (16, 64), 0), landed).astype(BF16)
        gather_b.s1()

    @step("a.s1")
    def _():
        wait_all(*state["la"])
        landed = ma[...].reshape(64, part)
        for q in range(4):
            sa[c, x, y, :, q * part : (q + 1) * part] = mm(fold(q, (16, 64), 0), landed).astype(BF16)
        gather_a.s1()

    pieces = [(0, 0, 4), (1, 0, 4), (2, 0, 4), (3, 0, 2), (3, 2, 2)]
    ring, ring_far, passed, stores = {}, {}, {}, []

    def slab_of(n, dz, cols=ALL):
        k, first, count = pieces[n]
        return w.at[c, k, pl.ds(first, count), rows_of(dz), cols]

    def z_start(n):
        own = slab_of(n, 0)
        ring[n] = net.send(own, own, net.at(dz=1)), net.send(own, own, net.at(dz=-1))
        ring_far[n], passed[n] = net.place(), net.place()
        net.sibling(own, passed[n])

    def z_forward(n):
        side = out_width // 2
        plus, minus = ring[n]
        plus.wait_recv()
        one = slab_of(n, -1, pl.ds(0, side))
        net.send(one, one, net.at(dz=1), ring_far[n])
        minus.wait_recv()
        two = slab_of(n, 1, pl.ds(side, side))
        net.send(two, two, net.at(dz=-1), ring_far[n])
        net.sibling(slab_of(n, -1), passed[n])
        net.sibling(slab_of(n, 1), passed[n])

    def z_end(n):
        last = slab_of(n, 2)
        wait_all(last, ring_far[n])
        net.sibling(last, passed[n])

    def multiply(n, i):
        k, first, count = pieces[n]
        if i == 0:
            wait_all(w.at[1 - c, k, pl.ds(first, count), pl.ds(SHARED, 256 - SHARED)], passed[n])
        count //= 2
        first += i * count

        def block(j, _):
            start = pl.multiple_of((k * RING + j) * 512, 512)
            one, two = w[0, k, j], w[1, k, j]
            cols, lo, hi = pl.ds(start, 512), pl.ds(start, 256), pl.ds(start + 256, 256)
            total[...] += mm(tok[c, :, lo], one) + mm(tok[c, :, hi], two)
            from_a = mm(back[...], sa[:, :, :, :, cols].reshape(512, 512))
            tg[:, lo] = (mm_last(cot[c], one) + from_a[:, :256]).astype(BF16)
            tg[:, hi] = (mm_last(cot[c], two) + from_a[:, 256:]).astype(BF16)
            return 0

        lax.fori_loop(first, first + count, block, 0)
        cols = pl.ds((k * RING + first) * 512, count * 512)
        store = pltpu.make_async_copy(tg.at[:, cols], token_grad.at[:, cols], local_sems.at[7 + len(stores)])
        store.start()
        stores.append(store)

    for n in range(len(pieces)):
        steps["z%d.go" % n] = lambda n=n: z_start(n)
        steps["z%d.fw" % n] = lambda n=n: z_forward(n)
        steps["z%d.en" % n] = lambda n=n: z_end(n)
        for i in range(2):
            steps["m%d.%d" % (n, i)] = lambda n=n, i=i: multiply(n, i)

    stack_b = lambda: sb[...].reshape(512, out_width)

    @step("back")
    def _():
        found = SCALE * mask[...] * mm_last(cot[c], stack_b())
        back[...] = found.astype(BF16)
        back_t[...] = found.T.astype(BF16).reshape(2, 256, rows)
        state["bx"] = net.send(back_t.at[1 - c], back_x, net.at(dc=1))

    def terms_a(i):
        if i == 0:
            state["tx"].wait_recv()
            state["cx"].wait_recv()
            state["bx"].wait_recv()

        def chunk(k, _):
            cols = pl.ds(pl.multiple_of(k * 512, 512), 512)
            found = mm(back_t[c], tok[c, :, cols]) + mm(back_x[...], tok[1 - c, :, cols])
            t_a[:, :, :, cols] = (found * row_scale).astype(BF16).reshape(4, 4, 16, 512)
            return 0

        count = width // 2048
        lax.fori_loop(i * count, (i + 1) * count, chunk, 0)

    for i in range(4):
        steps["T%d" % i] = lambda i=i: terms_a(i)

    def low_sum(i):
        def chunk(k, acc):
            cols = pl.ds(pl.multiple_of(k * 1024, 1024), 1024)
            return acc + mm_last(tok[c, :, cols], sa[:, :, :, :, cols].reshape(512, 1024))

        count = width // 2048
        return lax.fori_loop(i * count, (i + 1) * count, chunk, jnp.zeros((rows, 512), F32))

    @step("low0")
    def _():
        total[:, :512] = low_sum(0)

    @step("low1")
    def _():
        found = mask[...] * (total[:, :512] + low_sum(1))
        low[...] = found.astype(BF16)
        low_t[...] = found.T.astype(BF16).reshape(2, 256, rows)
        state["lx"] = net.send(low_t.at[1 - c], low_x, net.at(dc=1))

    @step("tot")
    def _():
        total[...] = SCALE * mm(low[...], stack_b())

    @step("tb")
    def _():
        state["lx"].wait_recv()
        found = mm(low_t[c], cot[c]) + mm(low_x[...], cot[1 - c])
        t_b[...] = (found * (SCALE * row_scale)).astype(BF16).reshape(4, 4, 16, out_width)

    def unfold(source, target, size):
        found = jnp.zeros((64, size), F32)
        for q in range(4):
            found += mm(fold(q, (64, 16), 1), source[:, q * size : (q + 1) * size])
        target[...] = found.astype(BF16).reshape(4, 16, size)

    @step("unf")
    def _():
        unfold(g_a, na, part)
        unfold(g_b, nb, part_b)

    @step("home")
    def _():
        state["ha"] = swap(net, na, ha)
        state["hb"] = swap(net, nb, hb)

    @step("homw")
    def _():
        wait_all(*state["ha"])
        wait_all(*state["hb"])
        home_a[...] = ha[...].reshape(64, part)
        home_b[...] = hb[...].reshape(64, part_b)

    @step("out")
    def _():
        output[...] = total[...].astype(BF16)

    pl.semaphore_wait(barrier, len(partners))
    for name in ORDER:
        steps[name]()
    for store in stores:
        store.wait()
    for copy in net.started[-SENDS:]:
        copy.wait_send()


def place_kernel(
    slot_table, home_a, home_b, found_output, found_grad, output, token_grad, grad_a, grad_b,
    held, held_grad, held_output, in_sems, out_sems,
):
    rows, owned = token_grad.shape[0], grad_b.shape[0]
    part, part_b = home_a.shape[1], home_b.shape[1]
    z = lax.axis_index("grp")
    count = rows // 8
    bands = [pl.ds(k * count, count) for k in range(8)]
    moves = [(found_grad.at[band], held_grad.at[band], token_grad.at[band]) for band in bands]
    moves.append((found_output, held_output, output))
    loads = [pltpu.make_async_copy(move[0], move[1], in_sems.at[k]) for k, move in enumerate(moves)]
    stores = [pltpu.make_async_copy(move[1], move[2], out_sems.at[k]) for k, move in enumerate(moves)]
    for load in loads:
        load.start()
    row = lax.broadcasted_iota(jnp.int32, (owned, 64), 1)
    adapter = lax.broadcasted_iota(jnp.int32, (owned, 64), 0)
    ids = wanted(slot_table, z, owned, row)
    for i in range(8):
        hits = pick(ids, row, adapter, i)
        cols = pl.ds(i * part, part)
        held[:, cols] = mm(hits, home_a[...]).astype(BF16)
        stores.append(pltpu.make_async_copy(held.at[:, cols], grad_a.at[:, cols], out_sems.at[9 + i]))
        stores[-1].start()
        loads[i].wait()
        stores[i].start()
        grad_b[:, i * part_b : (i + 1) * part_b] = mm(hits, home_b[...]).astype(BF16)
    loads[8].wait()
    stores[8].start()
    for store in stores:
        store.wait()


def local(tokens, tenant, slot_table, weight, adapter_a, adapter_b, cotangent):
    rows, width = tokens.shape
    out_width = weight.shape[1]
    owned = adapter_a.shape[0]
    part, part_b = width // 4, out_width // 4
    vmem, hbm = pl.BlockSpec(memory_space=pltpu.VMEM), pl.BlockSpec(memory_space=pltpu.HBM)
    smem = pl.BlockSpec(memory_space=pltpu.SMEM)
    buffer = lambda *shape, dtype=BF16: pltpu.VMEM(shape, dtype)
    found_output, found_grad, home_a, home_b = pl.pallas_call(
        kernel,
        name="exchange_and_multiply",
        out_shape=(
            jax.ShapeDtypeStruct((rows, out_width), BF16),
            jax.ShapeDtypeStruct((rows, width), BF16),
            jax.ShapeDtypeStruct((64, part), BF16),
            jax.ShapeDtypeStruct((64, part_b), BF16),
        ),
        in_specs=[smem, vmem, hbm, hbm, hbm, hbm, hbm],
        out_specs=(vmem, hbm, vmem, vmem),
        scratch_shapes=[
            buffer(2, 4, 4, 256, out_width),
            buffer(2, 4, 4, 16, width),
            buffer(2, 4, 4, 16, out_width),
            buffer(2, rows, width),
            buffer(2, rows, out_width),
            buffer(rows, width),
            buffer(owned, 2 * out_width),
            buffer(4, 4, 16, width),
            buffer(4, 4, 16, out_width),
            buffer(2, 6, 4, 16, part // 2),
            buffer(2, 6, 16, part // 2),
            buffer(2, 6, 4, 16, part // 2),
            buffer(2, 6, 16, part // 2),
            buffer(2, 6, 4, 16, part_b),
            buffer(2, 6, 16, part_b),
            buffer(16, width),
            buffer(16, out_width),
            buffer(rows, 512, dtype=F32),
            buffer(rows, 512),
            buffer(rows, 512),
            buffer(2, 256, rows),
            buffer(2, 256, rows),
            buffer(256, rows),
            buffer(256, rows),
            buffer(rows, out_width, dtype=F32),
            buffer(4, 16, part),
            buffer(4, 16, part_b),
            buffer(4, 16, part),
            buffer(4, 16, part_b),
            buffer(4, 16, part),
            buffer(4, 16, part_b),
            buffer(4, 16, part),
            buffer(4, 16, part_b),
            pltpu.SemaphoreType.DMA((17,)),
            pltpu.SemaphoreType.DMA((SENDS,)),
            pltpu.SemaphoreType.DMA((RECEIVES,)),
        ],
        compiler_params=pltpu.CompilerParams(
            collective_id=0, has_side_effects=True, vmem_limit_bytes=62 * 1024 * 1024
        ),
    )(slot_table, tenant.reshape(1, rows), tokens, weight, adapter_a, adapter_b, cotangent)

    return pl.pallas_call(
        place_kernel,
        name="place_results",
        out_shape=(
            jax.ShapeDtypeStruct((rows, out_width), BF16),
            jax.ShapeDtypeStruct((rows, width), BF16),
            jax.ShapeDtypeStruct(adapter_a.shape, BF16),
            jax.ShapeDtypeStruct(adapter_b.shape, BF16),
        ),
        in_specs=[smem, vmem, vmem, hbm, hbm],
        out_specs=(hbm, hbm, hbm, vmem),
        scratch_shapes=[
            buffer(owned, 2 * width),
            buffer(rows, width),
            buffer(rows, out_width),
            pltpu.SemaphoreType.DMA((9,)),
            pltpu.SemaphoreType.DMA((17,)),
        ],
        compiler_params=pltpu.CompilerParams(vmem_limit_bytes=62 * 1024 * 1024),
    )(slot_table, home_a, home_b, found_output, found_grad)


def solution(mesh):
    return jax.shard_map(
        local,
        mesh=mesh,
        in_specs=(
            P(("grp", "fsdp"), None),
            P(("grp", "fsdp")),
            P(),
            P("fsdp", None),
            P("grp", "fsdp"),
            P("grp", "fsdp"),
            P(("grp", "fsdp"), None),
        ),
        out_specs=(
            P(("grp", "fsdp"), None),
            P(("grp", "fsdp"), None),
            P("grp", "fsdp"),
            P("grp", "fsdp"),
        ),
        check_vma=False,
    )
```

time: 402 us -> 96.8 us (0.24)
  waiting for transfers between devices: 288 us -> 0 us
  Pallas kernels: 0 us -> 95.9 us
  matrix products: 60.9 us -> 0 us
  blocking collectives: 27.3 us -> 0 us
  between operations: 13.9 us -> 0.8 us
  local copies, waits for them, and re-layouts: 5.28 us -> 0 us
  starting transfers between devices: 4.35 us -> 0 us
    reduce_scatter x2 -> x0, waiting for transfers between devices: 143 us -> none  [the longest x1 84.8 us: local(): summed_a = lax.psum_scatter(term_a, 'fsdp', scatter_dimension=0, tiled=True)]
    all_gather x3 -> x0, waiting for transfers between devices: 141 us -> none  [the longest x1 64.9 us: local(): full_weight = lax.all_gather(weight, 'fsdp', axis=0, tiled=True)]
    pallas_call x0 -> x2, Pallas kernels: none -> 95.9 us  [the longest x1 89.3 us: local(): pl.pallas_call(kernel, name='exchange_and_multiply', out_shape=(jax.Shape...]
    dot_general x12 -> x0, matrix products: 60.9 us -> none  [the longest x3 21 us: contract_last(): lax.dot_general(left, right, (((1,), (1,)), ((), ())), preferred_element_...]
    all_to_all x3 -> x0, blocking collectives: 27.3 us -> none  [exchange(): lax.all_to_all(chosen.reshape(group_count, per_owner, -1), 'grp', 0, 0, t...]
    all_to_all x1 -> x0, starting transfers between devices: 4.14 us -> none  [exchange(): lax.all_to_all(chosen.reshape(group_count, per_owner, -1), 'grp', 0, 0, t...]
  transfers between devices with their start and end apart: 6 -> 0, of which waited for: 6 -> 0; matrix products, arithmetic and copies ran while one was open for 10% -> 0% of each run, Pallas kernels for 0% -> 0%
where the time goes in v3:
time: 96.8 us; the launch traced here: 96.7 us
  Pallas kernels  95.9 us (99%)
    pallas_call x1, Pallas kernels, local(): pl.pallas_call(kernel, name='exchange_and_multiply', out_shape=(jax.Shape...  89.3 us
    pallas_call x1, Pallas kernels, local(): pl.pallas_call(place_kernel, name='place_results', out_shape=(jax.ShapeDt...  6.56 us

profile of v3, /device:TPU:1, one launch (start us, length us, event | category | flops | bytes accessed | tf_op | source)
XLA Modules:
  0.0 96.7 jit_solution(363610886237045620)
XLA Ops:
  0.6 89.3 %exchange_and_multiply.1 = (bf16[256,1024]{1,0:T(8,128)(2,1)}, bf16[256,8192]{1,0:T(8,128)(2,1)}, bf16[64,2048]{1,0:T(8,128)(2,1)}, bf16[64,256]{1,0:T(8,128)(2,1)}) custom-call(s32[4,8]{1,0:T(4,128)} %slot_table.3, s32[1,256]{1,0:T(1,128)} %bitcast.1, bf16[256,8192]{1,0:T(8,128)(2,1)} %tokens.1, bf16[256,1024]{1,0:T(8,128)(2,1)} %weight.1, ...), custom_call_target="tpu_custom_call" | custom-call | tf_op jit(solution)/shard_map/exchange_and_multiply/pallas_call | solution.py:614
  89.9 6.6 %place_results.1 = (bf16[256,1024]{1,0:T(8,128)(2,1)}, bf16[256,8192]{1,0:T(8,128)(2,1)}, bf16[128,16384]{1,0:T(8,128)(2,1)}, bf16[128,2048]{1,0:T(8,128)(2,1)}) custom-call(s32[4,8]{1,0:T(4,128)} %slot_table.3, bf16[64,2048]{1,0:T(8,128)(2,1)} %get-tuple-element.8.home_a, bf16[64,256]{1,0:T(8,128)(2,1)} %get-tuple-element.9.home_b, ...), custom_call_target="tpu_custom_call" | custom-call | tf_op jit(solution)/shard_map/place_results/pallas_call | solution.py:668

commit v4 on v3

--- a/solution.py
+++ b/solution.py
@@ -9,18 +9,20 @@
 
 SCALE = 2.0
 RING = 4
-SENDS = 64
-RECEIVES = 120
+SENDS = 48
+RECEIVES = 128
 ORDER = (
-    "w.s1", "d.s1", "swapb", "b.s1", "w.s2", "swapa", "tokx", "d.s2", "b.s2", "w.s3", "a.s1", "b.s3",
-    "w.s4", "a.s2", "d.s3", "w.s5", "z0.go", "b.s4", "z1.go", "z2.go", "a.s3", "b.s5", "z0.fw", "d.s4",
-    "b.fin", "back", "a.s4", "T0", "T1", "T2", "r0.s1", "z1.fw", "a.s5", "T3", "r1.s1", "a.fin", "d.s5",
-    "low0", "z2.fw", "low1", "r0.s2", "z0.en", "z3.go", "tot", "tb", "d.fin", "q.s1", "r1.s2", "z1.en",
-    "m0.0", "m1.0", "z4.go", "z2.en", "m0.1", "q.s2", "r0.s3", "m2.0", "r1.s3", "z3.fw", "q.s3", "r0.s4",
-    "m1.1", "r1.s4", "q.s4", "z4.fw", "m2.1", "r0.s5", "z3.en", "r1.s5", "q.s5", "unf", "home", "m3.0",
-    "z4.en", "m3.1", "m4.0", "m4.1", "homw", "out",
+    "w.s1", "swapb", "swapa", "d.s1", "tokx", "b.s1", "w.s2", "d.s2", "b.s2", "a.s1", "w.s3", "z0.go",
+    "z1.go", "b.s3", "a.s2", "d.s3", "z0.fw", "b.s4", "a.s3", "w.s4", "z2.go", "z3.go", "b.s5", "z1.fw",
+    "z4.go", "b.fin", "back", "T0", "z5.go", "z0.en", "d.s4", "T1", "a.s4", "z1.en", "T2", "z2.fw", "r0.s1",
+    "a.s5", "z3.fw", "z4.fw", "d.s5", "T3", "z5.fw", "r1.s1", "w.s5", "a.fin", "low0", "z6.go", "z2.en",
+    "low1", "d.fin", "r0.s2", "tot", "m2.0", "z3.en", "m0.0", "z7.go", "tb", "q.s1", "r1.s2", "m0.1",
+    "m2.1", "m1.0", "z4.en", "m1.1", "z5.en", "m3.0", "q.s2", "m4.0", "z6.fw", "r0.s3", "m4.1", "m5.0",
+    "r1.s3", "m5.1", "q.s3", "r0.s4", "z7.fw", "m3.1", "r1.s4", "z6.en", "q.s4", "r0.s5", "hom0", "m6.0",
+    "r1.s5", "hom1", "q.s5", "z7.en", "homb", "m6.1", "m7.0", "m7.1", "homw", "out",
 )
-SHARED = 64
+SHARED = 16
+OFFSETS = (0, -1, 1, 2)
 MESH = pl.DeviceIdType.MESH
 ALL = slice(None)
 BF16 = jnp.bfloat16
@@ -89,8 +91,8 @@
 
 
 class Gather:
-    def __init__(self, net, ref, width, rows=ALL, to_sibling=True):
-        self.net, self.buffer, self.quarter, self.rows = net, ref, width // 4, rows
+    def __init__(self, net, ref, cut, to_sibling=True):
+        self.net, self.buffer, self.cut = net, ref, cut
         self.near, self.line = {}, {}
         self.far = [net.place(), net.place()]
         self.rest = [net.place(), net.place()]
@@ -98,8 +100,7 @@
 
     def ref(self, half, p, s, part, count):
         x, y = (p, s) if half == 0 else (s, p)
-        cols = pl.ds((half * 2 + part) * self.quarter, count * self.quarter)
-        return self.buffer.at[self.net.c, x, y, self.rows, cols]
+        return self.buffer.at[(self.net.c, x, y) + self.cut(half, part, count)]
 
     def at(self, half):
         return (self.net.x, self.net.y) if half == 0 else (self.net.y, self.net.x)
@@ -153,17 +154,14 @@
             self.hand(last)
 
     def fin(self):
-        wait_all(self.buffer.at[1 - self.net.c, :, :, self.rows], self.passed)
+        wait_all(self.buffer.at[(1 - self.net.c, ALL, ALL) + self.cut(None, 0, 2)], self.passed)
 
 
 class Scatter:
-    def __init__(self, net, terms, line_slots, block_slots, out, width, base=0):
-        self.net, self.terms, self.out, self.quarter, self.base = net, terms, out, width // 4, base
+    def __init__(self, net, terms, line_slots, block_slots, out, cols):
+        self.net, self.terms, self.out, self.cols = net, terms, out, cols
         self.line_slots, self.block_slots = line_slots, block_slots
         self.sems = [[[net.place() for _ in range(3)] for _ in range(2)] for _ in range(2)]
-
-    def cols(self, half, part):
-        return pl.ds(self.base + (half * 2 + part) * self.quarter, self.quarter)
 
     def index(self, half, p, s, part):
         x, y = (p, s) if half == 0 else (s, p)
@@ -305,23 +303,29 @@
     width, out_width = tokens.shape[1], weight.shape[1]
     rows = tokens.shape[0]
     owned = adapter_a.shape[0]
-    part = width // 4
-    part_b = out_width // 4
+    part_a, part_b = width // 4, out_width // 4
     row_scale = 1.0 / math.sqrt(rows * 2 * RING * RING)
-    shared, slab = pl.ds(0, SHARED), (256 - SHARED) // RING
-    rows_of = lambda dz: pl.ds(pl.multiple_of(SHARED + mod(z + dz) * slab, 16), slab)
-
-    loads = [
-        pltpu.make_async_copy(weight.at[rows_of(0)], w.at[c, x, y, rows_of(0)], local_sems.at[0]),
-        pltpu.make_async_copy(adapter_b, ab, local_sems.at[1]),
-        pltpu.make_async_copy(weight.at[shared], w.at[c, x, y, shared], local_sems.at[2]),
-        pltpu.make_async_copy(adapter_a.at[:, pl.ds(0, width)], tg.at[pl.ds(0, 128)], local_sems.at[3]),
-        pltpu.make_async_copy(adapter_a.at[:, pl.ds(width, width)], tg.at[pl.ds(128, 128)], local_sems.at[4]),
-        pltpu.make_async_copy(cotangent, cot.at[c], local_sems.at[5]),
-        pltpu.make_async_copy(tokens, tok.at[c], local_sems.at[6]),
-    ]
-    for load in loads:
-        load.start()
+    shared, rest, quarter = pl.ds(0, SHARED), pl.ds(SHARED, 128 - SHARED), out_width // 4
+
+    def slab_cols(dz, part=0, count=2):
+        start = mod(z + dz) * quarter + part * (quarter // 2)
+        return pl.ds(pl.multiple_of(start, quarter // 2), count * (quarter // 2))
+
+    loads = []
+
+    def load(source, target):
+        loads.append(pltpu.make_async_copy(source, target, local_sems.at[len(loads)]))
+        loads[-1].start()
+
+    for h in (0, 1):
+        load(weight.at[pl.ds(h * 128 + SHARED, 128 - SHARED), slab_cols(0)], w.at[c, x, y, h, rest, slab_cols(0)])
+    for h in (0, 1):
+        load(weight.at[pl.ds(h * 128, SHARED)], w.at[c, x, y, h, shared])
+    load(adapter_b, ab)
+    for r in (0, 1):
+        load(adapter_a.at[:, pl.ds(r * width, width)], tg.at[pl.ds(r * 128, 128)])
+    load(cotangent, cot.at[c])
+    load(tokens, tok.at[c])
 
     barrier = pltpu.get_barrier_semaphore()
     partners = [net.at(dx=1), net.at(dx=-1), net.at(dy=1), net.at(dy=-1), net.at(dz=1), net.at(dz=-1)]
@@ -343,18 +347,33 @@
             if hasattr(collective, stage):
                 steps[name + "." + stage] = getattr(collective, stage)
 
-    gather_w = Gather(net, w, out_width, rows=rows_of(0), to_sibling=False)
-    gather_d = Gather(net, w, out_width, rows=shared)
-    gather_a = Gather(net, sa, width)
-    gather_b = Gather(net, sb, out_width)
+    def cut_cols(width):
+        def cut(half, part, count):
+            return ALL, ALL if half is None else pl.ds((half * 2 + part) * (width // 4), count * (width // 4))
+
+        return cut
+
+    def cut_slab(half, part, count):
+        return half, rest, slab_cols(0, part, count)
+
+    def cut_shared(half, part, count):
+        return ALL if half is None else half, shared, pl.ds(part * (out_width // 2), count * (out_width // 2))
+
+    gather_w = Gather(net, w, cut_slab, to_sibling=False)
+    gather_d = Gather(net, w, cut_shared)
+    gather_a = Gather(net, sa, cut_cols(width))
+    gather_b = Gather(net, sb, cut_cols(out_width))
     stages("w", gather_w)
     stages("d", gather_d)
     stages("a", gather_a)
     stages("b", gather_b)
-    half = width // 2
-    stages("r0", Scatter(net, t_a, lx_0, ly_0, g_a, half))
-    stages("r1", Scatter(net, t_a, lx_1, ly_1, g_a, half, base=half))
-    stages("q", Scatter(net, t_b, lx_b, ly_b, g_b, out_width))
+
+    def wave(v):
+        return lambda half, part: pl.ds((half * 2 + part) * part_a + v * (part_a // 2), part_a // 2)
+
+    stages("r0", Scatter(net, t_a, lx_0, ly_0, g_a, wave(0)))
+    stages("r1", Scatter(net, t_a, lx_1, ly_1, g_a, wave(1)))
+    stages("q", Scatter(net, t_b, lx_b, ly_b, g_b, lambda half, part: pl.ds((half * 2 + part) * part_b, part_b)))
 
     row = lax.broadcasted_iota(jnp.int32, (64, owned), 0)
     adapter = lax.broadcasted_iota(jnp.int32, (64, owned), 1)
@@ -366,8 +385,8 @@
         slot_ids = slot_ids + jnp.where(slot == s, slot_table[z, s], 0)
     hit = jnp.where(slot_ids == tenant[...], 1.0, 0.0)
     mask[...] = jnp.concatenate([hit] * 32, axis=0).T
-    for load in loads[:3]:
-        load.wait()
+    for copy in loads[:5]:
+        copy.wait()
     chosen = jnp.zeros((64, part_b), F32)
     for i in range(8):
         chosen += mm(picks[i], ab[:, i * part_b : (i + 1) * part_b])
@@ -379,26 +398,26 @@
 
     @step("swapa")
     def _():
-        loads[3].wait()
-        loads[4].wait()
+        loads[5].wait()
+        loads[6].wait()
 
         def pick_a(k, _):
             cols = pl.ds(pl.multiple_of(k * 512, 512), 512)
             chosen = jnp.zeros((64, 512), F32)
             for i in range(8):
                 r, q = i // 4, i % 4
-                from_cols = pl.ds(pl.multiple_of(q * part + k * 512, 512), 512)
+                from_cols = pl.ds(pl.multiple_of(q * part_a + k * 512, 512), 512)
                 chosen += mm(picks[i], tg[r * 128 : (r + 1) * 128, from_cols])
             pa[:, :, cols] = chosen.astype(BF16).reshape(4, 16, 512)
             return 0
 
-        lax.fori_loop(0, part // 512, pick_a, 0)
+        lax.fori_loop(0, part_a // 512, pick_a, 0)
         state["la"] = swap(net, pa, ma)
 
     @step("tokx")
     def _():
-        loads[5].wait()
-        loads[6].wait()
+        loads[7].wait()
+        loads[8].wait()
         state["cx"] = net.sibling(cot.at[c])
         state["tx"] = net.sibling(tok.at[c])
 
@@ -413,65 +432,62 @@
     @step("a.s1")
     def _():
         wait_all(*state["la"])
-        landed = ma[...].reshape(64, part)
+        landed = ma[...].reshape(64, part_a)
         for q in range(4):
-            sa[c, x, y, :, q * part : (q + 1) * part] = mm(fold(q, (16, 64), 0), landed).astype(BF16)
+            sa[c, x, y, :, q * part_a : (q + 1) * part_a] = mm(fold(q, (16, 64), 0), landed).astype(BF16)
         gather_a.s1()
 
-    pieces = [(0, 0, 4), (1, 0, 4), (2, 0, 4), (3, 0, 2), (3, 2, 2)]
-    ring, ring_far, passed, stores = {}, {}, {}, []
-
-    def slab_of(n, dz, cols=ALL):
-        k, first, count = pieces[n]
-        return w.at[c, k, pl.ds(first, count), rows_of(dz), cols]
+    ring, ring_far, passed, stored = {}, {}, {}, {}
+
+    def place_of(n, i):
+        offset, h = OFFSETS[n // 2], n % 2
+        return (i, mod(y + offset)) if h == 0 else (mod(x + offset), i)
+
+    def slab_of(n, cols):
+        return w.at[(c,) + place_of(n, ALL) + (n % 2, rest, cols)]
 
     def z_start(n):
-        own = slab_of(n, 0)
+        own = slab_of(n, slab_cols(0))
         ring[n] = net.send(own, own, net.at(dz=1)), net.send(own, own, net.at(dz=-1))
         ring_far[n], passed[n] = net.place(), net.place()
         net.sibling(own, passed[n])
 
     def z_forward(n):
-        side = out_width // 2
         plus, minus = ring[n]
         plus.wait_recv()
-        one = slab_of(n, -1, pl.ds(0, side))
+        one = slab_of(n, slab_cols(-1, 0, 1))
         net.send(one, one, net.at(dz=1), ring_far[n])
         minus.wait_recv()
-        two = slab_of(n, 1, pl.ds(side, side))
+        two = slab_of(n, slab_cols(1, 1, 1))
         net.send(two, two, net.at(dz=-1), ring_far[n])
-        net.sibling(slab_of(n, -1), passed[n])
-        net.sibling(slab_of(n, 1), passed[n])
+        net.sibling(slab_of(n, slab_cols(-1)), passed[n])
+        net.sibling(slab_of(n, slab_cols(1)), passed[n])
 
     def z_end(n):
-        last = slab_of(n, 2)
+        last = slab_of(n, slab_cols(2))
         wait_all(last, ring_far[n])
         net.sibling(last, passed[n])
 
     def multiply(n, i):
-        k, first, count = pieces[n]
+        h = n % 2
         if i == 0:
-            wait_all(w.at[1 - c, k, pl.ds(first, count), pl.ds(SHARED, 256 - SHARED)], passed[n])
-        count //= 2
-        first += i * count
-
-        def block(j, _):
-            start = pl.multiple_of((k * RING + j) * 512, 512)
-            one, two = w[0, k, j], w[1, k, j]
-            cols, lo, hi = pl.ds(start, 512), pl.ds(start, 256), pl.ds(start + 256, 256)
-            total[...] += mm(tok[c, :, lo], one) + mm(tok[c, :, hi], two)
-            from_a = mm(back[...], sa[:, :, :, :, cols].reshape(512, 512))
-            tg[:, lo] = (mm_last(cot[c], one) + from_a[:, :256]).astype(BF16)
-            tg[:, hi] = (mm_last(cot[c], two) + from_a[:, 256:]).astype(BF16)
-            return 0
-
-        lax.fori_loop(first, first + count, block, 0)
-        cols = pl.ds((k * RING + first) * 512, count * 512)
-        store = pltpu.make_async_copy(tg.at[:, cols], token_grad.at[:, cols], local_sems.at[7 + len(stores)])
-        store.start()
-        stores.append(store)
-
-    for n in range(len(pieces)):
+            wait_all(w.at[(1 - c,) + place_of(n, ALL) + (h, rest)], passed[n])
+        places = [place_of(n, 2 * i), place_of(n, 2 * i + 1)]
+        cols, blocks = [], []
+        for px, py in places:
+            for core in (0, 1):
+                start = ((px * RING + py) * 2 + core) * 256 + h * 128
+                cols.append(pl.ds(pl.multiple_of(start, 128), 128))
+                blocks.append(w[core, px, py, h])
+        block = jnp.concatenate(blocks, axis=0)
+        total[...] += mm(jnp.concatenate([tok[c, :, at] for at in cols], axis=1), block)
+        from_a = mm(back[...], jnp.concatenate([sa[:, :, :, :, at].reshape(512, 128) for at in cols], axis=1))
+        found = (mm_last(cot[c], block) + from_a).astype(BF16)
+        for k, at in enumerate(cols):
+            tg[:, at] = found[:, k * 128 : (k + 1) * 128]
+            pltpu.make_async_copy(tg.at[:, at], token_grad.at[:, at], local_sems.at[n]).start()
+
+    for n in range(8):
         steps["z%d.go" % n] = lambda n=n: z_start(n)
         steps["z%d.fw" % n] = lambda n=n: z_forward(n)
         steps["z%d.en" % n] = lambda n=n: z_end(n)
@@ -494,13 +510,14 @@
             state["bx"].wait_recv()
 
         def chunk(k, _):
-            cols = pl.ds(pl.multiple_of(k * 512, 512), 512)
+            start = (k // 2) * part_a + (i // 2) * (part_a // 2) + (k % 2) * 512
+            cols = pl.ds(pl.multiple_of(start, 512), 512)
             found = mm(back_t[c], tok[c, :, cols]) + mm(back_x[...], tok[1 - c, :, cols])
             t_a[:, :, :, cols] = (found * row_scale).astype(BF16).reshape(4, 4, 16, 512)
             return 0
 
         count = width // 2048
-        lax.fori_loop(i * count, (i + 1) * count, chunk, 0)
+        lax.fori_loop(i % 2 * count, (i % 2 + 1) * count, chunk, 0)
 
     for i in range(4):
         steps["T%d" % i] = lambda i=i: terms_a(i)
@@ -534,27 +551,31 @@
         found = mm(low_t[c], cot[c]) + mm(low_x[...], cot[1 - c])
         t_b[...] = (found * (SCALE * row_scale)).astype(BF16).reshape(4, 4, 16, out_width)
 
-    def unfold(source, target, size):
-        found = jnp.zeros((64, size), F32)
+    def unfold(source, size, start, count):
+        found = jnp.zeros((64, count), F32)
         for q in range(4):
-            found += mm(fold(q, (64, 16), 1), source[:, q * size : (q + 1) * size])
-        target[...] = found.astype(BF16).reshape(4, 16, size)
-
-    @step("unf")
-    def _():
-        unfold(g_a, na, part)
-        unfold(g_b, nb, part_b)
-
-    @step("home")
-    def _():
-        state["ha"] = swap(net, na, ha)
+            found += mm(fold(q, (64, 16), 1), source[:, q * size + start : q * size + start + count])
+        return found.astype(BF16).reshape(4, 16, count)
+
+    def go_home(v):
+        cols = pl.ds(v * (part_a // 2), part_a // 2)
+        na[:, :, cols] = unfold(g_a, part_a, v * (part_a // 2), part_a // 2)
+        state["ha%d" % v] = swap(net, na.at[:, :, cols], ha.at[:, :, cols])
+
+    steps["hom0"] = lambda: go_home(0)
+    steps["hom1"] = lambda: go_home(1)
+
+    @step("homb")
+    def _():
+        nb[...] = unfold(g_b, part_b, 0, part_b)
         state["hb"] = swap(net, nb, hb)
 
     @step("homw")
     def _():
-        wait_all(*state["ha"])
+        wait_all(*state["ha0"])
+        wait_all(*state["ha1"])
         wait_all(*state["hb"])
-        home_a[...] = ha[...].reshape(64, part)
+        home_a[...] = ha[...].reshape(64, part_a)
         home_b[...] = hb[...].reshape(64, part_b)
 
     @step("out")
@@ -564,43 +585,54 @@
     pl.semaphore_wait(barrier, len(partners))
     for name in ORDER:
         steps[name]()
-    for store in stores:
-        store.wait()
+    for n in range(8):
+        wait_all(tg.at[:, pl.ds(0, 1024)], local_sems.at[n])
     for copy in net.started[-SENDS:]:
         copy.wait_send()
 
 
 def place_kernel(
     slot_table, home_a, home_b, found_output, found_grad, output, token_grad, grad_a, grad_b,
-    held, held_grad, held_output, in_sems, out_sems,
+    ha, hb, held, held_b, held_grad, held_output, in_sems, out_sems,
 ):
     rows, owned = token_grad.shape[0], grad_b.shape[0]
-    part, part_b = home_a.shape[1], home_b.shape[1]
+    part = home_a.shape[1]
     z = lax.axis_index("grp")
-    count = rows // 8
-    bands = [pl.ds(k * count, count) for k in range(8)]
-    moves = [(found_grad.at[band], held_grad.at[band], token_grad.at[band]) for band in bands]
+    count = rows // 4
+    bands = [pl.ds(k * count, count) for k in range(4)]
+    moves = [(home_a, ha, None), (home_b, hb, None)]
+    moves += [(found_grad.at[band], held_grad.at[band], token_grad.at[band]) for band in bands]
     moves.append((found_output, held_output, output))
     loads = [pltpu.make_async_copy(move[0], move[1], in_sems.at[k]) for k, move in enumerate(moves)]
-    stores = [pltpu.make_async_copy(move[1], move[2], out_sems.at[k]) for k, move in enumerate(moves)]
     for load in loads:
         load.start()
+    stores = []
+
+    def store(source, target):
+        stores.append(pltpu.make_async_copy(source, target, out_sems.at[len(stores)]))
+        stores[-1].start()
+
     row = lax.broadcasted_iota(jnp.int32, (owned, 64), 1)
     adapter = lax.broadcasted_iota(jnp.int32, (owned, 64), 0)
     ids = wanted(slot_table, z, owned, row)
+    loads[0].wait()
     for i in range(8):
-        hits = pick(ids, row, adapter, i)
         cols = pl.ds(i * part, part)
-        held[:, cols] = mm(hits, home_a[...]).astype(BF16)
-        stores.append(pltpu.make_async_copy(held.at[:, cols], grad_a.at[:, cols], out_sems.at[9 + i]))
-        stores[-1].start()
-        loads[i].wait()
-        stores[i].start()
-        grad_b[:, i * part_b : (i + 1) * part_b] = mm(hits, home_b[...]).astype(BF16)
-    loads[8].wait()
-    stores[8].start()
-    for store in stores:
-        store.wait()
+        held[:, cols] = mm(pick(ids, row, adapter, i), ha[...]).astype(BF16)
+        store(held.at[:, cols], grad_a.at[:, cols])
+        if i == 1:
+            for load, (_, source, target) in zip(loads[2:], moves[2:]):
+                load.wait()
+                store(source, target)
+    loads[1].wait()
+    line = lax.broadcasted_iota(jnp.int32, hb.shape, 0)
+    piece = (line % 2) * 4 + (line // 4) % 4
+    spread = jnp.concatenate([jnp.where(piece == i, hb[...], 0.0) for i in range(8)], axis=1)
+    hits = jnp.where(ids == adapter, 1.0, 0.0).astype(BF16)
+    held_b[...] = mm(hits, spread.astype(BF16)).astype(BF16)
+    store(held_b, grad_b)
+    for copy in stores:
+        copy.wait()
 
 
 def local(tokens, tenant, slot_table, weight, adapter_a, adapter_b, cotangent):
@@ -623,7 +655,7 @@
         in_specs=[smem, vmem, hbm, hbm, hbm, hbm, hbm],
         out_specs=(vmem, hbm, vmem, vmem),
         scratch_shapes=[
-            buffer(2, 4, 4, 256, out_width),
+            buffer(2, 4, 4, 2, 128, out_width),
             buffer(2, 4, 4, 16, width),
             buffer(2, 4, 4, 16, out_width),
             buffer(2, rows, width),
@@ -656,7 +688,7 @@
             buffer(4, 16, part_b),
             buffer(4, 16, part),
             buffer(4, 16, part_b),
-            pltpu.SemaphoreType.DMA((17,)),
+            pltpu.SemaphoreType.DMA((9,)),
             pltpu.SemaphoreType.DMA((SENDS,)),
             pltpu.SemaphoreType.DMA((RECEIVES,)),
         ],
@@ -674,14 +706,17 @@
             jax.ShapeDtypeStruct(adapter_a.shape, BF16),
             jax.ShapeDtypeStruct(adapter_b.shape, BF16),
         ),
-        in_specs=[smem, vmem, vmem, hbm, hbm],
-        out_specs=(hbm, hbm, hbm, vmem),
+        in_specs=[smem, hbm, hbm, hbm, hbm],
+        out_specs=(hbm, hbm, hbm, hbm),
         scratch_shapes=[
+            buffer(64, part),
+            buffer(64, part_b),
             buffer(owned, 2 * width),
+            buffer(owned, 2 * out_width),
             buffer(rows, width),
             buffer(rows, out_width),
-            pltpu.SemaphoreType.DMA((9,)),
-            pltpu.SemaphoreType.DMA((17,)),
+            pltpu.SemaphoreType.DMA((7,)),
+            pltpu.SemaphoreType.DMA((14,)),
         ],
         compiler_params=pltpu.CompilerParams(vmem_limit_bytes=62 * 1024 * 1024),
     )(slot_table, home_a, home_b, found_output, found_grad)

time: 96.8 us -> 92.7 us (0.958)
  Pallas kernels: 95.9 us -> 91.7 us
    pallas_call x1, Pallas kernels: 89.3 us -> 85.7 us  [local(): pl.pallas_call(kernel, name='exchange_and_multiply', out_shape=(jax.Shape...]
where the time goes in v4:
time: 92.7 us; the launch traced here: 92.5 us
  Pallas kernels  91.7 us (99%)
    pallas_call x1, Pallas kernels, local(): pl.pallas_call(kernel, name='exchange_and_multiply', out_shape=(jax.Shape...  85.7 us
    pallas_call x1, Pallas kernels, local(): pl.pallas_call(place_kernel, name='place_results', out_shape=(jax.ShapeDt...  6.03 us

profile of v4, /device:TPU:1, one launch (start us, length us, event | category | flops | bytes accessed | tf_op | source)
XLA Modules:
  0.0 92.5 jit_solution(5426288567207785621)
XLA Ops:
  0.6 85.7 %exchange_and_multiply.1 = (bf16[256,1024]{1,0:T(8,128)(2,1)}, bf16[256,8192]{1,0:T(8,128)(2,1)}, bf16[64,2048]{1,0:T(8,128)(2,1)}, bf16[64,256]{1,0:T(8,128)(2,1)}) custom-call(s32[4,8]{1,0:T(4,128)} %slot_table.3, s32[1,256]{1,0:T(1,128)} %bitcast.1, bf16[256,8192]{1,0:T(8,128)(2,1)} %tokens.1, bf16[256,1024]{1,0:T(8,128)(2,1)} %weight.1, ...), custom_call_target="tpu_custom_call" | custom-call | tf_op jit(solution)/shard_map/exchange_and_multiply/pallas_call | solution.py:646
  86.3 6.0 %place_results.1 = (bf16[256,1024]{1,0:T(8,128)(2,1)}, bf16[256,8192]{1,0:T(8,128)(2,1)}, bf16[128,16384]{1,0:T(8,128)(2,1)}, bf16[128,2048]{1,0:T(8,128)(2,1)}) custom-call(s32[4,8]{1,0:T(4,128)} %slot_table.3, bf16[64,2048]{1,0:T(8,128)(2,1)} %get-tuple-element.8.home_a, bf16[64,256]{1,0:T(8,128)(2,1)} %get-tuple-element.9.home_b, ...), custom_call_target="tpu_custom_call" | custom-call | tf_op jit(solution)/shard_map/place_results/pallas_call | solution.py:700

commit v5 on v4

--- a/solution.py
+++ b/solution.py
@@ -9,17 +9,18 @@
 
 SCALE = 2.0
 RING = 4
-SENDS = 48
-RECEIVES = 128
+SENDS = 40
+RECEIVES = 92
 ORDER = (
-    "w.s1", "swapb", "swapa", "d.s1", "tokx", "b.s1", "w.s2", "d.s2", "b.s2", "a.s1", "w.s3", "z0.go",
-    "z1.go", "b.s3", "a.s2", "d.s3", "z0.fw", "b.s4", "a.s3", "w.s4", "z2.go", "z3.go", "b.s5", "z1.fw",
-    "z4.go", "b.fin", "back", "T0", "z5.go", "z0.en", "d.s4", "T1", "a.s4", "z1.en", "T2", "z2.fw", "r0.s1",
-    "a.s5", "z3.fw", "z4.fw", "d.s5", "T3", "z5.fw", "r1.s1", "w.s5", "a.fin", "low0", "z6.go", "z2.en",
-    "low1", "d.fin", "r0.s2", "tot", "m2.0", "z3.en", "m0.0", "z7.go", "tb", "q.s1", "r1.s2", "m0.1",
-    "m2.1", "m1.0", "z4.en", "m1.1", "z5.en", "m3.0", "q.s2", "m4.0", "z6.fw", "r0.s3", "m4.1", "m5.0",
-    "r1.s3", "m5.1", "q.s3", "r0.s4", "z7.fw", "m3.1", "r1.s4", "z6.en", "q.s4", "r0.s5", "hom0", "m6.0",
-    "r1.s5", "hom1", "q.s5", "z7.en", "homb", "m6.1", "m7.0", "m7.1", "homw", "out",
+    "w.s1", "swapb", "swapa", "d.s1", "b.s1", "tokx", "mask", "w.s2", "d.s2", "a.s1", "b.s2", "w.s3", "z0.go",
+    "z1.go", "b.s3", "a.s2", "d.s3", "z0.fw", "b.s4", "a.s3", "w.s4", "z2.go", "z0.en", "b.s5", "z3.go",
+    "d.s4", "z1.fw", "z2.fw", "z4.go", "b.fin", "back", "T0", "a.s4", "T1", "T2", "d.s5", "z5.go", "T3",
+    "z1.en", "r1.s1", "r0.s1", "w.s5", "d.fin", "z2.en", "o1.0", "o2.0", "z3.fw", "o0.0", "o1.1", "z4.fw",
+    "a.s5", "o0.1", "a.fin", "z6.go", "low0", "low1", "r1.s2", "z3.en", "x0.0", "x1.0", "z4.en", "z5.fw",
+    "tb", "q.s1", "x2.0", "o4.0", "o3.0", "z7.go", "r0.s2", "x3.0", "x0.1", "x4.0", "x3.1", "q.s2", "r1.s3",
+    "z5.en", "o2.1", "o3.1", "x1.1", "z6.fw", "x2.1", "r0.s3", "o5.0", "q.s3", "x4.1", "r1.s4", "tot",
+    "z7.fw", "x5.0", "r0.s4", "x5.1", "z6.en", "q.s4", "o4.1", "o5.1", "r1.s5", "hom1", "o6.0", "x6.0",
+    "r0.s5", "hom0", "z7.en", "q.s5", "o6.1", "homb", "x6.1", "o7.0", "x7.0", "o7.1", "x7.1", "homw", "out",
 )
 SHARED = 16
 OFFSETS = (0, -1, 1, 2)
@@ -93,9 +94,7 @@
 class Gather:
     def __init__(self, net, ref, cut, to_sibling=True):
         self.net, self.buffer, self.cut = net, ref, cut
-        self.near, self.line = {}, {}
-        self.far = [net.place(), net.place()]
-        self.rest = [net.place(), net.place()]
+        self.near, self.far, self.line, self.rest = [[net.place(), net.place()] for _ in range(4)]
         self.passed = net.place() if to_sibling else None
 
     def ref(self, half, p, s, part, count):
@@ -116,15 +115,14 @@
         for half in (0, 1):
             p, s = self.at(half)
             own = self.ref(half, p, s, 0, 2)
-            self.near[half] = self.move(own, half, 1), self.move(own, half, -1)
+            self.move(own, half, 1, self.near[half])
+            self.move(own, half, -1, self.near[half])
 
     def s2(self):
         for half in (0, 1):
             p, s = self.at(half)
-            plus, minus = self.near[half]
-            plus.wait_recv()
+            wait_all(self.ref(half, pl.ds(0, 2), s, 0, 2), self.near[half])
             self.move(self.ref(half, mod(p - 1), s, 0, 1), half, 1, self.far[half])
-            minus.wait_recv()
             self.move(self.ref(half, mod(p + 1), s, 1, 1), half, -1, self.far[half])
 
     def s3(self):
@@ -132,16 +130,15 @@
             p, s = self.at(half)
             wait_all(self.ref(half, mod(p + 2), s, 0, 2), self.far[half])
             own = self.ref(half, ALL, s, 0, 2)
-            self.line[half] = self.move(own, 1 - half, 1), self.move(own, 1 - half, -1)
+            self.move(own, 1 - half, 1, self.line[half])
+            self.move(own, 1 - half, -1, self.line[half])
             self.hand(own)
 
     def s4(self):
         for half in (0, 1):
             _, s = self.at(half)
-            plus, minus = self.line[half]
-            plus.wait_recv()
+            wait_all(self.ref(half, ALL, pl.ds(0, 2), 0, 2), self.line[half])
             self.move(self.ref(half, ALL, mod(s - 1), 0, 1), 1 - half, 1, self.rest[half])
-            minus.wait_recv()
             self.move(self.ref(half, ALL, mod(s + 1), 1, 1), 1 - half, -1, self.rest[half])
             self.hand(self.ref(half, ALL, mod(s - 1), 0, 2))
             self.hand(self.ref(half, ALL, mod(s + 1), 0, 2))
@@ -161,7 +158,7 @@
     def __init__(self, net, terms, line_slots, block_slots, out, cols):
         self.net, self.terms, self.out, self.cols = net, terms, out, cols
         self.line_slots, self.block_slots = line_slots, block_slots
-        self.sems = [[[net.place() for _ in range(3)] for _ in range(2)] for _ in range(2)]
+        self.sems = [[[net.place(), net.place()] for _ in range(2)] for _ in range(2)]
 
     def index(self, half, p, s, part):
         x, y = (p, s) if half == 0 else (s, p)
@@ -175,9 +172,9 @@
         ahead, behind = self.net.plane(axis, 1), self.net.plane(axis, -1)
         at, slots, net = self.terms.at, slots.at, self.net
         net.send(at[block(mod(me + 2), 0)], slots[half, 0], ahead, sems[0])
-        net.send(at[block(mod(me + 2), 1)], slots[half, 1], behind, sems[1])
-        net.send(at[block(mod(me + 1), 1)], slots[half, 2], ahead, sems[2])
-        net.send(at[block(mod(me - 1), 0)], slots[half, 3], behind, sems[2])
+        net.send(at[block(mod(me + 2), 1)], slots[half, 1], behind, sems[0])
+        net.send(at[block(mod(me + 1), 1)], slots[half, 2], ahead, sems[1])
+        net.send(at[block(mod(me - 1), 0)], slots[half, 3], behind, sems[1])
 
     def add(self, block, slots):
         total = self.terms[block].astype(F32)
@@ -199,8 +196,8 @@
         for half in (0, 1):
             p, _ = self.at(half)
             sems = self.sems[0][half]
+            wait_all(self.line_slots.at[half, pl.ds(0, 2)], sems[0])
             for k, step in ((0, 1), (1, -1)):
-                wait_all(self.line_slots.at[half, k], sems[k])
                 target = mod(p + step)
 
                 def line(i, _, half=half, k=k, target=target):
@@ -213,13 +210,13 @@
                     self.terms.at[self.index(half, target, ALL, k)],
                     self.line_slots.at[half, 4 + k],
                     self.net.plane(half, step),
-                    sems[2],
+                    sems[1],
                 )
 
     def s3(self):
         for half in (0, 1):
             p, _ = self.at(half)
-            wait_all(self.line_slots.at[half, pl.ds(2, 4)], self.sems[0][half][2])
+            wait_all(self.line_slots.at[half, pl.ds(2, 4)], self.sems[0][half][1])
             for part in (0, 1):
 
                 def line(i, _, half=half, part=part, p=p):
@@ -241,21 +238,21 @@
         for half in (0, 1):
             p, s = self.at(half)
             sems = self.sems[1][half]
+            wait_all(self.block_slots.at[half, pl.ds(0, 2)], sems[0])
             for k, step in ((0, 1), (1, -1)):
-                wait_all(self.block_slots.at[half, k], sems[k])
                 block = self.index(half, p, mod(s + step), k)
                 self.terms[block] = self.add(block, [self.block_slots[half, k]]).astype(BF16)
                 self.net.send(
                     self.terms.at[block],
                     self.block_slots.at[half, 4 + k],
                     self.net.plane(1 - half, step),
-                    sems[2],
+                    sems[1],
                 )
 
     def s5(self):
         for half in (0, 1):
             p, s = self.at(half)
-            wait_all(self.block_slots.at[half, pl.ds(2, 4)], self.sems[1][half][2])
+            wait_all(self.block_slots.at[half, pl.ds(2, 4)], self.sems[1][half][1])
             for part in (0, 1):
                 block = self.index(half, p, s, part)
                 slots = [self.block_slots[half, 4 + part], self.block_slots[half, 3 - part]]
@@ -295,7 +292,7 @@
     slot_table, tenant, tokens, weight, adapter_a, adapter_b, cotangent,
     output, token_grad, home_a, home_b,
     w, sa, sb, tok, cot, tg, ab, t_a, t_b, lx_0, ly_0, lx_1, ly_1, lx_b, ly_b, g_a, g_b,
-    mask, back, low, back_t, low_t, back_x, low_x, total, pa, pb, ma, mb, ha, hb, na, nb,
+    mask, partial, back, low, back_t, low_t, back_x, low_x, total, held, pa, pb, ma, mb, ha, hb, na, nb,
     local_sems, send_sems, recv_sems,
 ):
     net = Net(send_sems, recv_sems)
@@ -375,31 +372,49 @@
     stages("r1", Scatter(net, t_a, lx_1, ly_1, g_a, wave(1)))
     stages("q", Scatter(net, t_b, lx_b, ly_b, g_b, lambda half, part: pl.ds((half * 2 + part) * part_b, part_b)))
 
-    row = lax.broadcasted_iota(jnp.int32, (64, owned), 0)
-    adapter = lax.broadcasted_iota(jnp.int32, (64, owned), 1)
-    ids = wanted(slot_table, z, owned, row)
-    picks = [pick(ids, row, adapter, i) for i in range(8)]
-    slot = lax.broadcasted_iota(jnp.int32, (16, rows), 0) // 2
-    slot_ids = jnp.zeros((16, rows), jnp.int32)
-    for s in range(8):
-        slot_ids = slot_ids + jnp.where(slot == s, slot_table[z, s], 0)
-    hit = jnp.where(slot_ids == tenant[...], 1.0, 0.0)
-    mask[...] = jnp.concatenate([hit] * 32, axis=0).T
-    for copy in loads[:5]:
-        copy.wait()
-    chosen = jnp.zeros((64, part_b), F32)
-    for i in range(8):
-        chosen += mm(picks[i], ab[:, i * part_b : (i + 1) * part_b])
-    pb[...] = chosen.astype(BF16).reshape(pb.shape)
+    @step("w.s1")
+    def _():
+        loads[0].wait()
+        loads[1].wait()
+        gather_w.s1()
+
+    @step("d.s1")
+    def _():
+        loads[2].wait()
+        loads[3].wait()
+        gather_d.s1()
+
+    def all_picks():
+        row = lax.broadcasted_iota(jnp.int32, (64, owned), 0)
+        adapter = lax.broadcasted_iota(jnp.int32, (64, owned), 1)
+        ids = wanted(slot_table, z, owned, row)
+        return [pick(ids, row, adapter, i) for i in range(8)]
+
+    @step("mask")
+    def _():
+        slot = lax.broadcasted_iota(jnp.int32, (16, rows), 0) // 2
+        slot_ids = jnp.zeros((16, rows), jnp.int32)
+        for s in range(8):
+            slot_ids = slot_ids + jnp.where(slot == s, slot_table[z, s], 0)
+        hit = jnp.where(slot_ids == tenant[...], 1.0, 0.0)
+        mask[...] = jnp.concatenate([hit] * 32, axis=0).T
+        total[...] = jnp.zeros_like(total)
 
     @step("swapb")
     def _():
+        loads[4].wait()
+        picks = state["picks"] = all_picks()
+        chosen = jnp.zeros((64, part_b), F32)
+        for i in range(8):
+            chosen += mm(picks[i], ab[:, i * part_b : (i + 1) * part_b])
+        pb[...] = chosen.astype(BF16).reshape(pb.shape)
         state["lb"] = swap(net, pb, mb)
 
     @step("swapa")
     def _():
         loads[5].wait()
         loads[6].wait()
+        picks = state["picks"]
 
         def pick_a(k, _):
             cols = pl.ds(pl.multiple_of(k * 512, 512), 512)
@@ -437,7 +452,7 @@
             sa[c, x, y, :, q * part_a : (q + 1) * part_a] = mm(fold(q, (16, 64), 0), landed).astype(BF16)
         gather_a.s1()
 
-    ring, ring_far, passed, stored = {}, {}, {}, {}
+    ring, ring_far, passed, stored = {}, {}, {}, []
 
     def place_of(n, i):
         offset, h = OFFSETS[n // 2], n % 2
@@ -448,16 +463,15 @@
 
     def z_start(n):
         own = slab_of(n, slab_cols(0))
-        ring[n] = net.send(own, own, net.at(dz=1)), net.send(own, own, net.at(dz=-1))
-        ring_far[n], passed[n] = net.place(), net.place()
+        ring[n], ring_far[n], passed[n] = net.place(), net.place(), net.place()
+        net.send(own, own, net.at(dz=1), ring[n])
+        net.send(own, own, net.at(dz=-1), ring[n])
         net.sibling(own, passed[n])
 
     def z_forward(n):
-        plus, minus = ring[n]
-        plus.wait_recv()
+        wait_all(w.at[(c,) + place_of(n, ALL) + (n % 2, rest, pl.ds(0, 2 * quarter))], ring[n])
         one = slab_of(n, slab_cols(-1, 0, 1))
         net.send(one, one, net.at(dz=1), ring_far[n])
-        minus.wait_recv()
         two = slab_of(n, slab_cols(1, 1, 1))
         net.send(two, two, net.at(dz=-1), ring_far[n])
         net.sibling(slab_of(n, slab_cols(-1)), passed[n])
@@ -468,19 +482,23 @@
         wait_all(last, ring_far[n])
         net.sibling(last, passed[n])
 
-    def multiply(n, i):
-        h = n % 2
-        if i == 0:
-            wait_all(w.at[(1 - c,) + place_of(n, ALL) + (h, rest)], passed[n])
-        places = [place_of(n, 2 * i), place_of(n, 2 * i + 1)]
-        cols, blocks = [], []
-        for px, py in places:
+    def blocks_of(n, i):
+        h, cols, blocks = n % 2, [], []
+        for px, py in (place_of(n, 2 * i), place_of(n, 2 * i + 1)):
             for core in (0, 1):
                 start = ((px * RING + py) * 2 + core) * 256 + h * 128
                 cols.append(pl.ds(pl.multiple_of(start, 128), 128))
                 blocks.append(w[core, px, py, h])
-        block = jnp.concatenate(blocks, axis=0)
+        return cols, jnp.concatenate(blocks, axis=0)
+
+    def multiply_out(n, i):
+        if i == 0:
+            wait_all(w.at[(1 - c,) + place_of(n, ALL) + (n % 2, rest)], passed[n])
+        cols, block = blocks_of(n, i)
         total[...] += mm(jnp.concatenate([tok[c, :, at] for at in cols], axis=1), block)
+
+    def multiply_back(n, i):
+        cols, block = blocks_of(n, i)
         from_a = mm(back[...], jnp.concatenate([sa[:, :, :, :, at].reshape(512, 128) for at in cols], axis=1))
         found = (mm_last(cot[c], block) + from_a).astype(BF16)
         for k, at in enumerate(cols):
@@ -492,7 +510,8 @@
         steps["z%d.fw" % n] = lambda n=n: z_forward(n)
         steps["z%d.en" % n] = lambda n=n: z_end(n)
         for i in range(2):
-            steps["m%d.%d" % (n, i)] = lambda n=n, i=i: multiply(n, i)
+            steps["o%d.%d" % (n, i)] = lambda n=n, i=i: multiply_out(n, i)
+            steps["x%d.%d" % (n, i)] = lambda n=n, i=i: multiply_back(n, i)
 
     stack_b = lambda: sb[...].reshape(512, out_width)
 
@@ -523,27 +542,23 @@
         steps["T%d" % i] = lambda i=i: terms_a(i)
 
     def low_sum(i):
-        def chunk(k, acc):
-            cols = pl.ds(pl.multiple_of(k * 1024, 1024), 1024)
-            return acc + mm_last(tok[c, :, cols], sa[:, :, :, :, cols].reshape(512, 1024))
-
-        count = width // 2048
-        return lax.fori_loop(i * count, (i + 1) * count, chunk, jnp.zeros((rows, 512), F32))
+        cols = pl.ds(i * (width // 2), width // 2)
+        return mm_last(tok[c, :, cols], sa[:, :, :, :, cols].reshape(512, width // 2))
 
     @step("low0")
     def _():
-        total[:, :512] = low_sum(0)
+        partial[...] = low_sum(0)
 
     @step("low1")
     def _():
-        found = mask[...] * (total[:, :512] + low_sum(1))
+        found = mask[...] * (partial[...] + low_sum(1))
         low[...] = found.astype(BF16)
         low_t[...] = found.T.astype(BF16).reshape(2, 256, rows)
         state["lx"] = net.send(low_t.at[1 - c], low_x, net.at(dc=1))
 
     @step("tot")
     def _():
-        total[...] = SCALE * mm(low[...], stack_b())
+        total[...] += SCALE * mm(low[...], stack_b())
 
     @step("tb")
     def _():
@@ -565,6 +580,10 @@
     steps["hom0"] = lambda: go_home(0)
     steps["hom1"] = lambda: go_home(1)
 
+    def store(source, target, k):
+        stored.append(pltpu.make_async_copy(source, target, local_sems.at[k]))
+        stored[-1].start()
+
     @step("homb")
     def _():
         nb[...] = unfold(g_b, part_b, 0, part_b)
@@ -575,16 +594,19 @@
         wait_all(*state["ha0"])
         wait_all(*state["ha1"])
         wait_all(*state["hb"])
-        home_a[...] = ha[...].reshape(64, part_a)
-        home_b[...] = hb[...].reshape(64, part_b)
+        store(ha, home_a, 8)
+        store(hb, home_b, 9)
 
     @step("out")
     def _():
-        output[...] = total[...].astype(BF16)
+        held[...] = total[...].astype(BF16)
+        store(held, output, 10)
 
     pl.semaphore_wait(barrier, len(partners))
     for name in ORDER:
         steps[name]()
+    for copy in stored:
+        copy.wait()
     for n in range(8):
         wait_all(tg.at[:, pl.ds(0, 1024)], local_sems.at[n])
     for copy in net.started[-SENDS:]:
@@ -596,7 +618,7 @@
     ha, hb, held, held_b, held_grad, held_output, in_sems, out_sems,
 ):
     rows, owned = token_grad.shape[0], grad_b.shape[0]
-    part = home_a.shape[1]
+    part = home_a.shape[2]
     z = lax.axis_index("grp")
     count = rows // 4
     bands = [pl.ds(k * count, count) for k in range(4)]
@@ -618,16 +640,17 @@
     loads[0].wait()
     for i in range(8):
         cols = pl.ds(i * part, part)
-        held[:, cols] = mm(pick(ids, row, adapter, i), ha[...]).astype(BF16)
+        held[:, cols] = mm(pick(ids, row, adapter, i), ha[...].reshape(64, part)).astype(BF16)
         store(held.at[:, cols], grad_a.at[:, cols])
         if i == 1:
             for load, (_, source, target) in zip(loads[2:], moves[2:]):
                 load.wait()
                 store(source, target)
     loads[1].wait()
-    line = lax.broadcasted_iota(jnp.int32, hb.shape, 0)
+    rows_b = hb[...].reshape(64, hb.shape[2])
+    line = lax.broadcasted_iota(jnp.int32, rows_b.shape, 0)
     piece = (line % 2) * 4 + (line // 4) % 4
-    spread = jnp.concatenate([jnp.where(piece == i, hb[...], 0.0) for i in range(8)], axis=1)
+    spread = jnp.concatenate([jnp.where(piece == i, rows_b, 0.0) for i in range(8)], axis=1)
     hits = jnp.where(ids == adapter, 1.0, 0.0).astype(BF16)
     held_b[...] = mm(hits, spread.astype(BF16)).astype(BF16)
     store(held_b, grad_b)
@@ -649,11 +672,11 @@
         out_shape=(
             jax.ShapeDtypeStruct((rows, out_width), BF16),
             jax.ShapeDtypeStruct((rows, width), BF16),
-            jax.ShapeDtypeStruct((64, part), BF16),
-            jax.ShapeDtypeStruct((64, part_b), BF16),
+            jax.ShapeDtypeStruct((4, 16, part), BF16),
+            jax.ShapeDtypeStruct((4, 16, part_b), BF16),
         ),
         in_specs=[smem, vmem, hbm, hbm, hbm, hbm, hbm],
-        out_specs=(vmem, hbm, vmem, vmem),
+        out_specs=(hbm, hbm, hbm, hbm),
         scratch_shapes=[
             buffer(2, 4, 4, 2, 128, out_width),
             buffer(2, 4, 4, 16, width),
@@ -673,6 +696,7 @@
             buffer(16, width),
             buffer(16, out_width),
             buffer(rows, 512, dtype=F32),
+            buffer(rows, 512, dtype=F32),
             buffer(rows, 512),
             buffer(rows, 512),
             buffer(2, 256, rows),
@@ -680,6 +704,7 @@
             buffer(256, rows),
             buffer(256, rows),
             buffer(rows, out_width, dtype=F32),
+            buffer(rows, out_width),
             buffer(4, 16, part),
             buffer(4, 16, part_b),
             buffer(4, 16, part),
@@ -688,7 +713,7 @@
             buffer(4, 16, part_b),
             buffer(4, 16, part),
             buffer(4, 16, part_b),
-            pltpu.SemaphoreType.DMA((9,)),
+            pltpu.SemaphoreType.DMA((11,)),
             pltpu.SemaphoreType.DMA((SENDS,)),
             pltpu.SemaphoreType.DMA((RECEIVES,)),
         ],
@@ -709,8 +734,8 @@
         in_specs=[smem, hbm, hbm, hbm, hbm],
         out_specs=(hbm, hbm, hbm, hbm),
         scratch_shapes=[
-            buffer(64, part),
-            buffer(64, part_b),
+            buffer(4, 16, part),
+            buffer(4, 16, part_b),
             buffer(owned, 2 * width),
             buffer(owned, 2 * out_width),
             buffer(rows, width),

time: 92.7 us -> 92.1 us (level)
  no operation moved by 1% of the time
where the time goes in v5:
time: 92.1 us; the launch traced here: 91.9 us
  Pallas kernels  91.1 us (99%)
    pallas_call x1, Pallas kernels, local(): pl.pallas_call(kernel, name='exchange_and_multiply', out_shape=(jax.Shape...  85.1 us
    pallas_call x1, Pallas kernels, local(): pl.pallas_call(place_kernel, name='place_results', out_shape=(jax.ShapeDt...  6.03 us

profile of v5, /device:TPU:1, one launch (start us, length us, event | category | flops | bytes accessed | tf_op | source)
XLA Modules:
  0.0 91.9 jit_solution(3133371332300963062)
XLA Ops:
  0.6 85.1 %exchange_and_multiply.1 = (bf16[256,1024]{1,0:T(8,128)(2,1)}, bf16[256,8192]{1,0:T(8,128)(2,1)}, bf16[4,16,2048]{2,1,0:T(8,128)(2,1)}, bf16[4,16,256]{2,1,0:T(8,128)(2,1)}) custom-call(s32[4,8]{1,0:T(4,128)} %slot_table.3, s32[1,256]{1,0:T(1,128)} %bitcast.1, bf16[256,8192]{1,0:T(8,128)(2,1)} %tokens.1, bf16[256,1024]{1,0:T(8,128)(2,1)} %weight.1, ...), custom_call_target="tpu_custom_call" | custom-call | tf_op jit(solution)/shard_map/exchange_and_multiply/pallas_call | solution.py:669
  85.7 6.0 %place_results.1 = (bf16[256,1024]{1,0:T(8,128)(2,1)}, bf16[256,8192]{1,0:T(8,128)(2,1)}, bf16[128,16384]{1,0:T(8,128)(2,1)}, bf16[128,2048]{1,0:T(8,128)(2,1)}) custom-call(s32[4,8]{1,0:T(4,128)} %slot_table.3, bf16[4,16,2048]{2,1,0:T(8,128)(2,1)} %get-tuple-element.8.home_a, bf16[4,16,256]{2,1,0:T(8,128)(2,1)} %get-tuple-element.9.home_b, ...), custom_call_target="tpu_custom_call" | custom-call | tf_op jit(solution)/shard_map/place_results/pallas_call | solution.py:725

commit v6 on v5

--- a/solution.py
+++ b/solution.py
@@ -315,7 +315,7 @@
         loads[-1].start()
 
     for h in (0, 1):
-        load(weight.at[pl.ds(h * 128 + SHARED, 128 - SHARED), slab_cols(0)], w.at[c, x, y, h, rest, slab_cols(0)])
+        load(weight.at[pl.ds(h * 128 + SHARED, 128 - SHARED)], w.at[c, x, y, h, rest])
     for h in (0, 1):
         load(weight.at[pl.ds(h * 128, SHARED)], w.at[c, x, y, h, shared])
     load(adapter_b, ab)
@@ -458,29 +458,38 @@
         offset, h = OFFSETS[n // 2], n % 2
         return (i, mod(y + offset)) if h == 0 else (mod(x + offset), i)
 
-    def slab_of(n, cols):
-        return w.at[(c,) + place_of(n, ALL) + (n % 2, rest, cols)]
+    def line_of(n, cols):
+        count = 3 if n < 2 else 4
+        return w.at[(c,) + place_of(n, pl.ds(0, count)) + (n % 2, rest, cols)]
+
+    def slabs_of(n, cols):
+        if n >= 2:
+            return [line_of(n, cols)]
+        others = [mod((x if n == 0 else y) + k) for k in (1, 2, 3)]
+        return [w.at[(c,) + place_of(n, i) + (n % 2, rest, cols)] for i in others]
 
     def z_start(n):
-        own = slab_of(n, slab_cols(0))
         ring[n], ring_far[n], passed[n] = net.place(), net.place(), net.place()
-        net.send(own, own, net.at(dz=1), ring[n])
-        net.send(own, own, net.at(dz=-1), ring[n])
-        net.sibling(own, passed[n])
+        for own in slabs_of(n, slab_cols(0)):
+            net.send(own, own, net.at(dz=1), ring[n])
+            net.send(own, own, net.at(dz=-1), ring[n])
+            net.sibling(own, passed[n])
+        if n < 2:
+            net.sibling(w.at[c, x, y, n % 2, rest], passed[n])
 
     def z_forward(n):
-        wait_all(w.at[(c,) + place_of(n, ALL) + (n % 2, rest, pl.ds(0, 2 * quarter))], ring[n])
-        one = slab_of(n, slab_cols(-1, 0, 1))
-        net.send(one, one, net.at(dz=1), ring_far[n])
-        two = slab_of(n, slab_cols(1, 1, 1))
-        net.send(two, two, net.at(dz=-1), ring_far[n])
-        net.sibling(slab_of(n, slab_cols(-1)), passed[n])
-        net.sibling(slab_of(n, slab_cols(1)), passed[n])
+        wait_all(line_of(n, pl.ds(0, 2 * quarter)), ring[n])
+        for one in slabs_of(n, slab_cols(-1, 0, 1)):
+            net.send(one, one, net.at(dz=1), ring_far[n])
+        for two in slabs_of(n, slab_cols(1, 1, 1)):
+            net.send(two, two, net.at(dz=-1), ring_far[n])
+        for slab in slabs_of(n, slab_cols(-1)) + slabs_of(n, slab_cols(1)):
+            net.sibling(slab, passed[n])
 
     def z_end(n):
-        last = slab_of(n, slab_cols(2))
-        wait_all(last, ring_far[n])
-        net.sibling(last, passed[n])
+        wait_all(line_of(n, slab_cols(2)), ring_far[n])
+        for last in slabs_of(n, slab_cols(2)):
+            net.sibling(last, passed[n])
 
     def blocks_of(n, i):
         h, cols, blocks = n % 2, [], []

time: 92.1 us -> 92.2 us (level)
  no operation moved by 1% of the time
where the time goes in v6:
time: 92.2 us; the launch traced here: 92 us
  Pallas kernels  91.2 us (99%)
    pallas_call x1, Pallas kernels, local(): pl.pallas_call(kernel, name='exchange_and_multiply', out_shape=(jax.Shape...  85.2 us
    pallas_call x1, Pallas kernels, local(): pl.pallas_call(place_kernel, name='place_results', out_shape=(jax.ShapeDt...  6 us

profile of v6, /device:TPU:1, one launch (start us, length us, event | category | flops | bytes accessed | tf_op | source)
XLA Modules:
  0.0 92.0 jit_solution(9739417815806739882)
XLA Ops:
  0.6 85.2 %exchange_and_multiply.1 = (bf16[256,1024]{1,0:T(8,128)(2,1)}, bf16[256,8192]{1,0:T(8,128)(2,1)}, bf16[4,16,2048]{2,1,0:T(8,128)(2,1)}, bf16[4,16,256]{2,1,0:T(8,128)(2,1)}) custom-call(s32[4,8]{1,0:T(4,128)} %slot_table.3, s32[1,256]{1,0:T(1,128)} %bitcast.1, bf16[256,8192]{1,0:T(8,128)(2,1)} %tokens.1, bf16[256,1024]{1,0:T(8,128)(2,1)} %weight.1, ...), custom_call_target="tpu_custom_call" | custom-call | tf_op jit(solution)/shard_map/exchange_and_multiply/pallas_call | solution.py:678
  85.9 6.0 %place_results.1 = (bf16[256,1024]{1,0:T(8,128)(2,1)}, bf16[256,8192]{1,0:T(8,128)(2,1)}, bf16[128,16384]{1,0:T(8,128)(2,1)}, bf16[128,2048]{1,0:T(8,128)(2,1)}) custom-call(s32[4,8]{1,0:T(4,128)} %slot_table.3, bf16[4,16,2048]{2,1,0:T(8,128)(2,1)} %get-tuple-element.8.home_a, bf16[4,16,256]{2,1,0:T(8,128)(2,1)} %get-tuple-element.9.home_b, ...), custom_call_target="tpu_custom_call" | custom-call | tf_op jit(solution)/shard_map/place_results/pallas_call | solution.py:734
